TPU v7x, 512 devices: a whole 4x4x16 slice. The times are simulated.
512 devices in a mesh: chan: 64 (over y, x, z_hi, core), tm: 8 (over z_lo).
Axes of the slice: x: 4, y: 4, z: 16 (z_hi: 2, z_lo: 8; z = z_hi * 8 + z_lo), core: 2. Of those that a mesh axis runs over, the one named last changes fastest.
Arguments:
- raw: bfloat16 [8192, 32, 3072], P('chan', 'tm')
- alive: int32 [8192], P('chan'), may hold values 0 or 1
- use: int32 [32], P('tm'), may hold values 0 or 1
Outputs:
- stack: bfloat16 [8192, 128, 256], P(('chan', 'tm'))
All inputs are finite; a program needn't handle non-finite values. No bound on the sum of `alive` or of `use` on one device may be relied on, other than what follows from the above.
Results may differ from a plain program's by a relative error of at most 0.0067.
Values may be sent and summed in bfloat16 or wider, within the bound.
No kernel may reach another device: no remote copies, remote signals or barrier semaphores. Data moves between devices by JAX's collectives and lax.ppermute only.
A program may use at most 128 MiB of HBM per device.

v0:
```python
import math

import jax
import jax.numpy as jnp
from jax import lax
from jax.sharding import PartitionSpec as P

BINS = 128
OFFS = 128


def from_behind(value, axis, steps):
    count = lax.axis_size(axis)
    leading, last = (max(0, -steps), min(count, count - steps))
    return lax.ppermute(value, axis, [(source, source + steps) for source in range(leading, last)])


def make_basis(nsamp, bins):
    times = jnp.arange(nsamp, dtype=jnp.int32)[:, None]
    freqs = jnp.arange(1, bins + 1, dtype=jnp.int32)[None, :]
    phase = (times * freqs % nsamp).astype(jnp.float32) * (2.0 * math.pi / nsamp)
    scale = 1.0 / math.sqrt(nsamp)
    return (jnp.concatenate([jnp.cos(phase), -jnp.sin(phase)], axis=1) * scale).astype(jnp.bfloat16)


def band_rows(values, rows, keep):
    width = values.shape[1]
    depth = values.shape[2]
    flat = values.reshape(rows * width, depth)
    flat = jnp.pad(flat, ((0, rows), (0, 0)))
    return flat.reshape(rows, width + 1, depth)[:, :keep]


def pair_dot(left, right):
    return jnp.einsum("isf,jsf->ijf", left, right, preferred_element_type=jnp.float32)


def shards(raw, alive, use):
    channels, seg_local, nsamp = raw.shape
    groups = lax.axis_size("tm")
    total_segs = seg_local * groups
    basis = make_basis(nsamp, BINS)
    signal = raw.astype(jnp.float32)
    meansq = jnp.mean(signal * signal, axis=-1, keepdims=True)
    normed = (signal * lax.rsqrt(meansq + 1e-06)).astype(jnp.bfloat16)
    spec = jnp.dot(
        normed.reshape(channels * seg_local, nsamp), basis, preferred_element_type=jnp.float32
    )
    spec = spec.reshape(channels, seg_local, 2 * BINS)
    sq = spec[..., :BINS] ** 2 + spec[..., BINS:] ** 2
    partial_power = jnp.sum(sq.reshape(channels, seg_local, BINS // 16, 16), axis=(1, 3))
    power = lax.psum(partial_power, "tm") / (16.0 * total_segs)
    scale = jnp.repeat(lax.rsqrt(power + 1e-06), 16, axis=1)
    scale = jnp.concatenate([scale, scale], axis=1)
    white = (
        spec
        * scale[:, None, :]
        * alive.astype(jnp.float32)[:, None, None]
        * use.astype(jnp.float32)[None, :, None]
    )
    white = white.astype(jnp.bfloat16)
    sub = channels // groups
    mine = lax.all_to_all(white, "tm", split_axis=0, concat_axis=1, tiled=True)
    count = (OFFS + sub - 2) // sub
    pieces = [mine]
    for step in range(1, count + 1):
        pieces.append(from_behind(mine, ("chan", "tm"), -step))
    extended = jnp.concatenate(pieces, axis=0)
    own = extended[:sub]
    re_own, im_own = (own[..., :BINS], own[..., BINS:])
    re_ext, im_ext = (extended[..., :BINS], extended[..., BINS:])
    real = pair_dot(re_own, re_ext) + pair_dot(im_own, im_ext)
    imag = pair_dot(im_own, re_ext) - pair_dot(re_own, im_ext)
    both = jnp.concatenate([band_rows(real, sub, OFFS), band_rows(imag, sub, OFFS)], axis=-1)
    return (both * (1.0 / total_segs)).astype(jnp.bfloat16)


def solution(mesh):
    in_specs = (P("chan", "tm", None), P("chan"), P("tm"))
    out_specs = P(("chan", "tm"), None, None)
    return jax.shard_map(shards, mesh=mesh, in_specs=in_specs, out_specs=out_specs, check_vma=False)
```

profile of v0, /device:TPU:4, one launch (start us, length us, event | category | flops | bytes accessed | tf_op | source)
XLA Modules:
  0.0 250.6 jit_solution(11765624798463709308)
XLA Ops:
  0.0 6.4 %fusion.25 = (f32[3072,128]{1,0:T(8,128)S(1)}, f32[3072,128]{1,0:T(8,128)S(1)}) fusion(s32[128]{0:T(128)S(1)} %iota_add_fusion), kind=kLoop, calls=%fused_computation.29 | loop fusion | flops 3932160 | bytes 3146240 | tf_op jit(solution)/shard_map/cos | solution.py:23
  9.9 2.2 fusion.3
  12.3 36.3 %psum.7 = f32[128,8]{0,1:T(8,128)S(1)} all-reduce(f32[128,8]{0,1:T(8,128)S(1)} %bitcast_reduce_fusion), channel_id=1, replica_groups=mesh['chan'=64,'tm'=8] {'tm'}, use_global_device_ids=true, to_apply=%region_3.4 | all-reduce | flops 1024 | bytes 8192 | tf_op jit(solution)/shard_map/psum | solution.py:52
  49.1 16.9 %all_to_all.18 = bf16[128,4,256]{2,1,0:T(4,128)(2,1)S(1)} all-to-all(bf16[128,4,256]{2,1,0:T(4,128)(2,1)S(1)} %copy.113), channel_id=1, replica_groups=mesh['chan'=64,'tm'=8] {'tm'}, dimensions={0} | all-to-all | bytes 524288 | tf_op jit(solution)/shard_map/all_to_all | solution.py:63
  72.6 9.8 %collective-permute-start.3 = (bf16[16,32,256]{2,1,0:T(8,128)(2,1)}, bf16[16,32,256]{2,1,0:T(8,128)(2,1)}, u32[]{:S(2)}, u32[]{:S(2)}) collective-permute-start(bf16[16,32,256]{2,1,0:T(8,128)(2,1)} %copy.116), channel_id=1, source_target_pairs={{4,0},{5,1},{6,2},{7,3},{8,4},{9,5},{10,6},{11,7},{12,8},{13,9},{1... | collective-permute-start | bytes 786440 | tf_op jit(solution)/shard_map/ppermute | solution.py:15
  82.4 6.4 %collective-permute-start.4 = (bf16[16,32,256]{2,1,0:T(8,128)(2,1)}, bf16[16,32,256]{2,1,0:T(8,128)(2,1)}, u32[]{:S(2)}, u32[]{:S(2)}) collective-permute-start(bf16[16,32,256]{2,1,0:T(8,128)(2,1)} %copy.116), channel_id=1, source_target_pairs={{5,0},{6,1},{7,2},{8,3},{9,4},{10,5},{11,6},{12,7},{13,8},{14,9},{... | collective-permute-start | bytes 786440 | tf_op jit(solution)/shard_map/ppermute | solution.py:15
  88.8 2.6 %collective-permute-start.5 = (bf16[16,32,256]{2,1,0:T(8,128)(2,1)}, bf16[16,32,256]{2,1,0:T(8,128)(2,1)}, u32[]{:S(2)}, u32[]{:S(2)}) collective-permute-start(bf16[16,32,256]{2,1,0:T(8,128)(2,1)} %copy.116), channel_id=1, source_target_pairs={{6,0},{7,1},{8,2},{9,3},{10,4},{11,5},{12,6},{13,7},{14,8},{15,9},... | collective-permute-start | bytes 786440 | tf_op jit(solution)/shard_map/ppermute | solution.py:15
  91.5 5.5 %collective-permute-start.6 = (bf16[16,32,256]{2,1,0:T(8,128)(2,1)}, bf16[16,32,256]{2,1,0:T(8,128)(2,1)}, u32[]{:S(2)}, u32[]{:S(2)}) collective-permute-start(bf16[16,32,256]{2,1,0:T(8,128)(2,1)} %copy.116), channel_id=1, source_target_pairs={{7,0},{8,1},{9,2},{10,3},{11,4},{12,5},{13,6},{14,7},{15,8},{16,9}... | collective-permute-start | bytes 786440 | tf_op jit(solution)/shard_map/ppermute | solution.py:15
  96.9 3.8 %collective-permute-done.2 = bf16[16,32,256]{2,1,0:T(8,128)(2,1)S(1)} collective-permute-done((bf16[16,32,256]{2,1,0:T(8,128)(2,1)}, bf16[16,32,256]{2,1,0:T(8,128)(2,1)S(1)}, u32[]{:S(2)}, u32[]{:S(2)}) %collective-permute-start.2) | collective-permute-done | bytes 262176 | tf_op jit(solution)/shard_map/ppermute | solution.py:15
  100.8 5.3 %collective-permute-start.7 = (bf16[16,32,256]{2,1,0:T(8,128)(2,1)}, bf16[16,32,256]{2,1,0:T(8,128)(2,1)}, u32[]{:S(2)}, u32[]{:S(2)}) collective-permute-start(bf16[16,32,256]{2,1,0:T(8,128)(2,1)} %copy.116), channel_id=1, source_target_pairs={{8,0},{9,1},{10,2},{11,3},{12,4},{13,5},{14,6},{15,7},{16,8},{17,9... | collective-permute-start | bytes 786440 | tf_op jit(solution)/shard_map/ppermute | solution.py:15
  106.1 3.0 %copy.124 = bf16[16,32,256]{0,1,2:T(8,128)(2,1)S(1)} copy(bf16[16,32,256]{2,0,1:T(8,128)(2,1)S(1)} %bitcast.23) | data formatting | bytes 524288 | tf_op jit(solution)/shard_map/all_to_all | solution.py:63
  110.1 3.8 %copy.125 = bf16[16,32,256]{0,1,2:T(8,128)(2,1)} copy(bf16[16,32,256]{2,1,0:T(8,128)(2,1)S(1)} %collective-permute-done) | data formatting | bytes 524288 | tf_op jit(solution)/shard_map/ppermute | solution.py:15
  113.9 5.2 %copy.126 = bf16[16,32,256]{0,1,2:T(8,128)(2,1)} copy(bf16[16,32,256]{2,1,0:T(8,128)(2,1)} %copy-done.4) | data formatting | bytes 524288 | tf_op jit(solution)/shard_map/ppermute | solution.py:15
  119.1 3.7 %copy.127 = bf16[16,32,256]{0,1,2:T(8,128)(2,1)} copy(bf16[16,32,256]{2,1,0:T(8,128)(2,1)S(1)} %copy-done.6) | data formatting | bytes 524288 | tf_op jit(solution)/shard_map/ppermute | solution.py:15
  122.8 5.2 %copy.128 = bf16[16,32,256]{0,1,2:T(8,128)(2,1)} copy(bf16[16,32,256]{2,1,0:T(8,128)(2,1)} %collective-permute-done.3) | data formatting | bytes 524288 | tf_op jit(solution)/shard_map/ppermute | solution.py:15
  128.0 63.9 %collective-permute-done.4 = bf16[16,32,256]{2,1,0:T(8,128)(2,1)} collective-permute-done((bf16[16,32,256]{2,1,0:T(8,128)(2,1)}, bf16[16,32,256]{2,1,0:T(8,128)(2,1)}, u32[]{:S(2)}, u32[]{:S(2)}) %collective-permute-start.4) | collective-permute-done | bytes 262176 | tf_op jit(solution)/shard_map/ppermute | solution.py:15
  191.9 5.1 %copy.129 = bf16[16,32,256]{0,1,2:T(8,128)(2,1)} copy(bf16[16,32,256]{2,1,0:T(8,128)(2,1)} %collective-permute-done.4) | data formatting | bytes 524288 | tf_op jit(solution)/shard_map/ppermute | solution.py:15
  197.0 5.1 %copy.130 = bf16[16,32,256]{0,1,2:T(8,128)(2,1)} copy(bf16[16,32,256]{2,1,0:T(8,128)(2,1)} %collective-permute-done.5) | data formatting | bytes 524288 | tf_op jit(solution)/shard_map/ppermute | solution.py:15
  202.2 5.2 %copy.131 = bf16[16,32,256]{0,1,2:T(8,128)(2,1)} copy(bf16[16,32,256]{2,1,0:T(8,128)(2,1)} %collective-permute-done.6) | data formatting | bytes 524288 | tf_op jit(solution)/shard_map/ppermute | solution.py:15
  207.4 5.2 %copy.132 = bf16[16,32,256]{0,1,2:T(8,128)(2,1)} copy(bf16[16,32,256]{2,1,0:T(8,128)(2,1)} %collective-permute-done.7) | data formatting | bytes 524288 | tf_op jit(solution)/shard_map/ppermute | solution.py:15
  212.5 18.9 %concatenate.14 = bf16[144,32,256]{0,1,2:T(8,128)(2,1)} concatenate(bf16[16,32,256]{0,1,2:T(8,128)(2,1)S(1)} %copy.124, bf16[16,32,256]{0,1,2:T(8,128)(2,1)} %copy.125, bf16[16,32,256]{0,1,2:T(8,128)(2,1)} %copy.126, bf16[16,32,256]{0,1,2:T(8,128)(2,1)} %copy.127, bf16[16,32,256]{0,1,2:T(8,128)(2,1)} %copy.128, bf16[16,32,256]{0,1,2:T(8,128)(2,1)} %copy.129, ...), dimensions={0} | concatenate | bytes 4718592 | tf_op jit(solution)/shard_map/concatenate | solution.py:68
  231.4 2.2 fusion.6
  236.5 2.7 %copy.135 = f32[16,144,128]{2,1,0:T(8,128)} copy(f32[16,144,128]{1,0,2:T(8,128)} %add_bitcast_fusion) | data formatting | bytes 2359296 | tf_op jit(solution)/shard_map/add | solution.py:72
  242.7 3.4 %subtract_bitcast_fusion = f32[16,144,128]{1,0,2:T(8,128)} fusion(f32[128,144,16]{1,2,0:T(8,128)S(1)} %fusion.8, bf16[16,32,128]{1,0,2:T(8,128)(2,1)S(1)} %copy-done.3, bf16[144,32,256]{0,1,2:T(8,128)(2,1)} %concatenate.14), kind=kOutput, calls=%fused_computation.11 | convolution fusion | flops 19169280 | bytes 4587520 | tf_op jit(solution)/shard_map/isf,jsf->ijf/dot_general | solution.py:35
  (59 shorter events, 22.6 us)
Async XLA Ops:
  0.0 6.4 %copy-start.1 = (bf16[128,4,3072]{2,1,0:T(4,128)(2,1)S(1)}, bf16[128,4,3072]{2,1,0:T(4,128)(2,1)}, u32[]{:S(2)}) copy-start(bf16[128,4,3072]{2,1,0:T(4,128)(2,1)} %param.3) | copy-start | bytes 9437188
  9.9 38.8 %copy-start.7 = (s32[128]{0:T(128)S(1)}, s32[128]{0:T(128)}, u32[]{:S(2)}) copy-start(s32[128]{0:T(128)} %param.4) | copy-start | bytes 1540
  9.9 38.8 %copy-start.8 = (s32[4]{0:T(128)S(1)}, s32[4]{0:T(128)}, u32[]{:S(2)}) copy-start(s32[4]{0:T(128)} %param.5) | copy-start | bytes 52
  66.9 21.9 %collective-permute-start = (bf16[16,32,256]{2,1,0:T(8,128)(2,1)}, bf16[16,32,256]{2,1,0:T(8,128)(2,1)S(1)}, u32[]{:S(2)}, u32[]{:S(2)}) collective-permute-start(bf16[16,32,256]{2,1,0:T(8,128)(2,1)} %copy.116), channel_id=1, source_target_pairs={{1,0},{2,1},{3,2},{4,3},{5,4},{6,5},{7,6},{8,7},{9,8},{10,9},{11,1... | collective-permute-start | bytes 786440 | tf_op jit(solution)/shard_map/ppermute | solution.py:15
  68.8 22.7 %collective-permute-start.1 = (bf16[16,32,256]{2,1,0:T(8,128)(2,1)}, bf16[16,32,256]{2,1,0:T(8,128)(2,1)S(1)}, u32[]{:S(2)}, u32[]{:S(2)}) collective-permute-start(bf16[16,32,256]{2,1,0:T(8,128)(2,1)} %copy.116), channel_id=1, source_target_pairs={{2,0},{3,1},{4,2},{5,3},{6,4},{7,5},{8,6},{9,7},{10,8},{11,9},{12,... | collective-permute-start | bytes 786440 | tf_op jit(solution)/shard_map/ppermute | solution.py:15
  70.7 30.0 %collective-permute-start.2 = (bf16[16,32,256]{2,1,0:T(8,128)(2,1)}, bf16[16,32,256]{2,1,0:T(8,128)(2,1)S(1)}, u32[]{:S(2)}, u32[]{:S(2)}) collective-permute-start(bf16[16,32,256]{2,1,0:T(8,128)(2,1)} %copy.116), channel_id=1, source_target_pairs={{3,0},{4,1},{5,2},{6,3},{7,4},{8,5},{9,6},{10,7},{11,8},{12,9},{13... | collective-permute-start | bytes 786440 | tf_op jit(solution)/shard_map/ppermute | solution.py:15
  72.6 50.2 %collective-permute-start.3 = (bf16[16,32,256]{2,1,0:T(8,128)(2,1)}, bf16[16,32,256]{2,1,0:T(8,128)(2,1)}, u32[]{:S(2)}, u32[]{:S(2)}) collective-permute-start(bf16[16,32,256]{2,1,0:T(8,128)(2,1)} %copy.116), channel_id=1, source_target_pairs={{4,0},{5,1},{6,2},{7,3},{8,4},{9,5},{10,6},{11,7},{12,8},{13,9},{1... | collective-permute-start | bytes 786440 | tf_op jit(solution)/shard_map/ppermute | solution.py:15
  82.4 109.5 %collective-permute-start.4 = (bf16[16,32,256]{2,1,0:T(8,128)(2,1)}, bf16[16,32,256]{2,1,0:T(8,128)(2,1)}, u32[]{:S(2)}, u32[]{:S(2)}) collective-permute-start(bf16[16,32,256]{2,1,0:T(8,128)(2,1)} %copy.116), channel_id=1, source_target_pairs={{5,0},{6,1},{7,2},{8,3},{9,4},{10,5},{11,6},{12,7},{13,8},{14,9},{... | collective-permute-start | bytes 786440 | tf_op jit(solution)/shard_map/ppermute | solution.py:15
  88.8 108.2 %collective-permute-start.5 = (bf16[16,32,256]{2,1,0:T(8,128)(2,1)}, bf16[16,32,256]{2,1,0:T(8,128)(2,1)}, u32[]{:S(2)}, u32[]{:S(2)}) collective-permute-start(bf16[16,32,256]{2,1,0:T(8,128)(2,1)} %copy.116), channel_id=1, source_target_pairs={{6,0},{7,1},{8,2},{9,3},{10,4},{11,5},{12,6},{13,7},{14,8},{15,9},... | collective-permute-start | bytes 786440 | tf_op jit(solution)/shard_map/ppermute | solution.py:15
  91.5 17.6 %copy-start.4 = (bf16[16,32,256]{2,1,0:T(8,128)(2,1)}, bf16[16,32,256]{2,1,0:T(8,128)(2,1)S(1)}, u32[]{:S(2)}) copy-start(bf16[16,32,256]{2,1,0:T(8,128)(2,1)S(1)} %collective-permute-done.1) | copy-start | bytes 786436
  91.5 110.7 %collective-permute-start.6 = (bf16[16,32,256]{2,1,0:T(8,128)(2,1)}, bf16[16,32,256]{2,1,0:T(8,128)(2,1)}, u32[]{:S(2)}, u32[]{:S(2)}) collective-permute-start(bf16[16,32,256]{2,1,0:T(8,128)(2,1)} %copy.116), channel_id=1, source_target_pairs={{7,0},{8,1},{9,2},{10,3},{11,4},{12,5},{13,6},{14,7},{15,8},{16,9}... | collective-permute-start | bytes 786440 | tf_op jit(solution)/shard_map/ppermute | solution.py:15
  100.8 5.3 %copy-start.5 = (bf16[16,32,256]{2,1,0:T(8,128)(2,1)}, bf16[16,32,256]{2,1,0:T(8,128)(2,1)S(1)}, u32[]{:S(2)}) copy-start(bf16[16,32,256]{2,1,0:T(8,128)(2,1)S(1)} %collective-permute-done.2) | copy-start | bytes 786436
  100.8 106.6 %collective-permute-start.7 = (bf16[16,32,256]{2,1,0:T(8,128)(2,1)}, bf16[16,32,256]{2,1,0:T(8,128)(2,1)}, u32[]{:S(2)}, u32[]{:S(2)}) collective-permute-start(bf16[16,32,256]{2,1,0:T(8,128)(2,1)} %copy.116), channel_id=1, source_target_pairs={{8,0},{9,1},{10,2},{11,3},{12,4},{13,5},{14,6},{15,7},{16,8},{17,9... | collective-permute-start | bytes 786440 | tf_op jit(solution)/shard_map/ppermute | solution.py:15
  109.6 121.8 %copy-start.2 = (bf16[16,32,128]{1,0,2:T(8,128)(2,1)}, bf16[16,32,128]{1,0,2:T(8,128)(2,1)S(1)}, u32[]{:S(2)}) copy-start(bf16[16,32,128]{1,0,2:T(8,128)(2,1)S(1)} %copy.138) | copy-start | bytes 393220
  113.9 5.2 %copy-start.6 = (bf16[16,32,256]{2,1,0:T(8,128)(2,1)S(1)}, bf16[16,32,256]{2,1,0:T(8,128)(2,1)}, u32[]{:S(2)}) copy-start(bf16[16,32,256]{2,1,0:T(8,128)(2,1)} %copy-done.5) | copy-start | bytes 786436
  231.4 2.8 %copy-start = (bf16[144,32,256]{0,1,2:T(8,128)(2,1)S(1)}, bf16[144,32,256]{0,1,2:T(8,128)(2,1)}, u32[]{:S(2)}) copy-start(bf16[144,32,256]{0,1,2:T(8,128)(2,1)} %concatenate.14) | copy-start | bytes 7077892
  241.7 1.0 copy-start.3
  248.2 1.2 slice-start
where the time goes:
time: 252 us; the launch traced here: 251 us
  local copies, waits for them, and re-layouts  72.7 us (29%)
  waiting for transfers between devices  67.7 us (27%)
  blocking collectives  53.2 us (21%)
  starting transfers between devices  35.3 us (14%)
  other arithmetic  11.3 us (4%)
  matrix products  9.96 us (4%)
    ppermute x8, waiting for transfers between devices, from_behind(): lax.ppermute(value, axis, [(source, source + steps) for source in range(l...  67.7 us
    ppermute x8, local copies, waits for them, and re-layouts, from_behind(): lax.ppermute(value, axis, [(source, source + steps) for source in range(l...  38.5 us
    psum x1, blocking collectives, shards(): power = lax.psum(partial_power, 'tm') / (16.0 * total_segs)  36.3 us
    ppermute x8, starting transfers between devices, from_behind(): lax.ppermute(value, axis, [(source, source + steps) for source in range(l...  35.3 us
    concatenate x1, local copies, waits for them, and re-layouts, shards(): extended = jnp.concatenate(pieces, axis=0)  18.9 us
    all_to_all x1, blocking collectives, shards(): mine = lax.all_to_all(white, 'tm', split_axis=0, concat_axis=1, tiled=True)  16.9 us
    dot_general x4, matrix products, pair_dot(): jnp.einsum('isf,jsf->ijf', left, right, preferred_element_type=jnp.float32)  7.79 us
    cos x1, other arithmetic, make_basis(): jnp.cos(phase)  6.39 us
  transfers between devices with their start and end apart: 8, of which 2 were waited for; matrix products, arithmetic and copies ran while one was open for 15% of the time, Pallas kernels for 0%

commit v1 on v0

v1 whole, which is shorter than its diff:
```python
import functools
import math

import jax
import jax.numpy as jnp
import numpy as np
from jax import lax
from jax.experimental import pallas as pl
from jax.experimental.pallas import tpu as pltpu
from jax.sharding import Mesh
from jax.sharding import PartitionSpec as P

BINS = 128
OFFS = 128
GROUP = 16
QUADS = 4
BATCHES = 2
F32 = jnp.float32
BF16 = jnp.bfloat16
VMEM = pl.BlockSpec(memory_space=pltpu.VMEM)
SMEM = pl.BlockSpec(memory_space=pltpu.SMEM)


def basis_columns(nsamp):
    times = np.arange(nsamp, dtype=np.int32)[:, None]
    freqs = np.arange(1, BINS + 1, dtype=np.int32)[None, :]
    phase = (times * freqs % nsamp).astype(np.float32) * np.float32(2.0 * math.pi / nsamp)
    scale = np.float32(1.0 / math.sqrt(nsamp))
    both = np.stack([np.cos(phase) * scale, -np.sin(phase) * scale], axis=-1)
    return jnp.asarray(both.reshape(nsamp, 2 * BINS), BF16)


def dot_nt(left, right):
    return lax.dot_general(left, right, (((1,), (1,)), ((), ())), preferred_element_type=F32)


def pack_kernel(use_ref, spec_ref, out_ref, scratch):
    segs, _, width = spec_ref.shape
    eye = (
        lax.broadcasted_iota(jnp.int32, (width, width), 0)
        == lax.broadcasted_iota(jnp.int32, (width, width), 1)
    ).astype(F32).astype(BF16)
    for seg in range(segs):
        scratch[pl.ds(seg, width, stride=segs), :] = dot_nt(eye, spec_ref[seg])
    rows = width * segs // QUADS
    seg_of_row = lax.broadcasted_iota(jnp.int32, (16, 128), 0) % segs
    flags = jnp.zeros((16, 128), F32)
    for seg in range(segs):
        flags = jnp.where(seg_of_row == seg, use_ref[seg].astype(F32), flags)
    for quad in range(QUADS):
        out_ref[quad, :16, :] = flags.astype(BF16)
        out_ref[quad, 16:, :] = scratch[quad * rows : (quad + 1) * rows, :].astype(BF16)


def stack_kernel(total_segs, par_ref, near_ref, far_ref, halo_ref, nflag_ref, fflag_ref, out_ref, scratch):
    half, swap, quad = par_ref[0], par_ref[1], par_ref[2]
    srcs, depth, width = near_ref.shape
    own_rows = 64

    def power(*parts):
        total = jnp.zeros((1, width), F32)
        for part in parts:
            value = part.astype(F32)
            total += jnp.sum(value * value, axis=(0, 1))[None, :]
        return lax.rsqrt(total * (1.0 / (GROUP * total_segs)) + 1e-06)

    own_scale = power(near_ref[...], far_ref[...])
    halo_scale = power(halo_ref[0], halo_ref[1])
    col_scale = jnp.concatenate([own_scale, halo_scale], axis=1) * (1.0 / total_segs)
    pick = lax.broadcasted_iota(jnp.int32, (own_rows, width), 1) == (
        64 * half + 63 - lax.broadcasted_iota(jnp.int32, (own_rows, width), 0)
    )
    row_scale = jnp.sum(jnp.where(pick, own_scale, 0.0), axis=1, keepdims=True)
    scale = row_scale * col_scale
    pick = pick.astype(F32).astype(BF16)

    row = lax.broadcasted_iota(jnp.int32, (128, 128), 0)
    col = lax.broadcasted_iota(jnp.int32, (128, 128), 1)
    flags = jnp.concatenate(
        [nflag_ref[src] for src in range(srcs)] + [fflag_ref[src] for src in range(srcs)], axis=0
    ).astype(F32)
    place = []
    for bin_ in range(2):
        keep = (col // 8) % 2 == bin_
        sign = jnp.where((col // 4) % 2 == 0, 1.0, -1.0)
        place.append(jnp.where(keep & (row == col), flags, 0.0))
        place.append(jnp.where(keep & (row == (col ^ 4)), flags * sign, 0.0))
    place = jnp.concatenate(place, axis=1).astype(BF16)

    def fill(which):
        for pair in range(GROUP // 2):
            rows = slice(16 * pair, 16 * pair + 16)
            own = jnp.concatenate(
                [near_ref[src, rows, :] for src in range(srcs)] + [far_ref[src, rows, :] for src in range(srcs)], axis=0
            )
            behind = jnp.concatenate(
                [halo_ref[swap, src, rows, :] for src in range(srcs)]
                + [halo_ref[1 - swap, src, rows, :] for src in range(srcs)],
                axis=0,
            )
            turned = dot_nt(pick, own).astype(BF16)
            left = jnp.dot(turned, place, preferred_element_type=F32).astype(BF16)
            left = jnp.concatenate([left[:, 128 * k : 128 * k + 128] for k in range(4)], axis=0)
            right = jnp.concatenate([own, behind], axis=1)
            both = jnp.dot(left, right, preferred_element_type=F32)
            for bin_ in range(2):
                for part in range(2):
                    k = 2 * bin_ + part
                    block = both[64 * k : 64 * k + 64] * scale
                    block = pltpu.roll(block, 193 - 64 * which, 1, stride=1, stride_axis=0)
                    scratch[pl.ds(part * 16 + 2 * pair + bin_, own_rows, stride=32), :] = block[:, :OFFS]

    for which in range(2):
        pl.when(half == which)(functools.partial(fill, which))
    for slot in range(QUADS):
        start = pl.multiple_of((3 - (quad ^ slot)) * 512, 512)
        out_ref[slot] = scratch[pl.ds(start, 512), :].astype(BF16)


def turn_kernel(par_ref, *refs):
    parts, out_ref, scratch = refs[:-2], refs[-2], refs[-1]
    quad = par_ref[2]
    count = out_ref.shape[0]
    eye = (
        lax.broadcasted_iota(jnp.int32, (128, 128), 0) == lax.broadcasted_iota(jnp.int32, (128, 128), 1)
    ).astype(F32).astype(BF16)
    for index, ref in enumerate(parts):
        batch, slot = index // QUADS, index % QUADS
        group = (quad ^ slot) * BATCHES + batch
        for row in range(count):
            for part in range(2):
                start = pl.multiple_of(part * 128 + GROUP * group, GROUP)
                scratch[count - 1 - row, pl.ds(start, GROUP), :] = ref[(2 * row + part) * 16 : (2 * row + part) * 16 + 16, :]
    for row in range(count):
        out_ref[row] = dot_nt(eye, scratch[row]).astype(BF16)


def shards(raw, alive, use):
    channels, seg_local, nsamp = raw.shape
    chans = lax.axis_size("chan")
    total_segs = seg_local * lax.axis_size("h") * lax.axis_size("q")
    axes = ("chan", "h", "q")
    me = lax.axis_index("chan")
    par = jnp.stack([lax.axis_index("h"), me % 2, lax.axis_index("q")]).astype(jnp.int32)

    meansq = jnp.mean(jnp.square(raw.astype(F32)), axis=-1, keepdims=True)
    scale = lax.rsqrt(meansq + 1e-06)
    spec = jnp.einsum("csn,nv->csv", raw, basis_columns(nsamp), preferred_element_type=F32)
    spec = jnp.where(scale > 0, spec * scale, 0.0) * alive.astype(F32)[:, None, None]
    spec = jnp.transpose(spec.astype(BF16), (1, 0, 2))
    rows = 2 * BINS * seg_local // QUADS
    message = pl.pallas_call(
        pack_kernel,
        out_shape=jax.ShapeDtypeStruct((QUADS, 16 + rows, channels), BF16),
        in_specs=[SMEM, VMEM],
        out_specs=VMEM,
        scratch_shapes=[pltpu.VMEM((rows * QUADS, channels), F32)],
        name="pack",
    )(use, spec)

    near = lax.all_to_all(message, "q", 0, 0, tiled=True)

    def index(chan, half, quad):
        return (chan * 2 + half) * QUADS + quad

    places = [(c, h, q) for c in range(chans) for h in range(2) for q in range(QUADS)]
    across = [(index(c, h, q), index(c, 1 - h, q)) for c, h, q in places]
    behind = [(index(c, h, q), index(c - 1, h if c % 2 else 1 - h, q)) for c, h, q in places if c > 0]
    batch_rows = rows // BATCHES
    near_parts = [near[:, : 16 + batch_rows], near[:, 16 + batch_rows :]]
    far_parts = [lax.ppermute(part, axes, across) for part in near_parts]
    near_flags, far_flags = near_parts[0][:, :16], far_parts[0][:, :16]
    near_parts[0], far_parts[0] = near_parts[0][:, 16:], far_parts[0][:, 16:]

    pieces = []
    for batch in range(BATCHES):
        own = jnp.stack([near_parts[batch], far_parts[batch]])
        halo = lax.ppermute(own, axes, behind)
        stacked = pl.pallas_call(
            functools.partial(stack_kernel, total_segs),
            out_shape=jax.ShapeDtypeStruct((QUADS, 512, OFFS), BF16),
            in_specs=[SMEM] + [VMEM] * 5,
            out_specs=VMEM,
            scratch_shapes=[pltpu.VMEM((512 * QUADS, OFFS), F32)],
            cost_estimate=pl.CostEstimate(flops=2 * 8 * 256 * 256 * 256, bytes_accessed=2**20, transcendentals=0),
            name="stack",
        )(par, near_parts[batch], far_parts[batch], halo, near_flags, far_flags)
        pieces.append(stacked[0])
        for slot in range(1, QUADS):
            pairs = [(index(c, h, q), index(c, h, q ^ slot)) for c, h, q in places]
            pieces.append(lax.ppermute(stacked[slot], axes, pairs))

    sub = channels // (2 * QUADS)
    steps = 4
    return pl.pallas_call(
        turn_kernel,
        out_shape=jax.ShapeDtypeStruct((sub, OFFS, 2 * BINS), BF16),
        grid=(steps,),
        in_specs=[SMEM] + [pl.BlockSpec((512 // steps, OFFS), lambda step: (steps - 1 - step, 0))] * len(pieces),
        out_specs=pl.BlockSpec((sub // steps, OFFS, 2 * BINS), lambda step: (step, 0, 0)),
        scratch_shapes=[pltpu.VMEM((sub // steps, 2 * BINS, OFFS), BF16)],
        name="turn",
    )(par, *pieces)


def solution(mesh):
    chans, groups = mesh.devices.shape
    fine = Mesh(mesh.devices.reshape(chans, 2, groups // 2), ("chan", "h", "q"))
    in_specs = (P("chan", ("h", "q"), None), P("chan"), P(("h", "q")))
    out_specs = P(("chan", "h", "q"), None, None)
    return jax.shard_map(shards, mesh=fine, in_specs=in_specs, out_specs=out_specs, check_vma=False)
```

time: 252 us -> 127 us (0.50)
  the two profiles are of different devices: /device:TPU:4 before, /device:TPU:25 now
where the time goes in v1:
time: 127 us; the launch traced here: 126 us
  starting transfers between devices  56.4 us (44%)
  waiting for transfers between devices  23.9 us (19%)
  Pallas kernels  14.5 us (11%)
  blocking collectives  13 us (10%)
  local copies, waits for them, and re-layouts  8.32 us (7%)
  other arithmetic  5.28 us (4%)
  matrix products  4.1 us (3%)
    ppermute x6, starting transfers between devices, shards(): pieces.append(lax.ppermute(stacked[slot], axes, pairs))  34.9 us
    ppermute x2, waiting for transfers between devices, shards(): far_parts = [lax.ppermute(part, axes, across) for part in near_parts]  18.3 us
    all_to_all x1, blocking collectives, shards(): near = lax.all_to_all(message, 'q', 0, 0, tiled=True)  13 us
    ppermute x2, starting transfers between devices, shards(): halo = lax.ppermute(own, axes, behind)  10.8 us
    ppermute x2, starting transfers between devices, shards(): far_parts = [lax.ppermute(part, axes, across) for part in near_parts]  10.7 us
    pallas_call x2, Pallas kernels, shards(): pl.pallas_call(functools.partial(stack_kernel, total_segs), out_shape=jax...  8.79 us
    ppermute x6, waiting for transfers between devices, shards(): pieces.append(lax.ppermute(stacked[slot], axes, pairs))  5.2 us
    dot_general x1, matrix products, shards(): jnp.einsum('csn,nv->csv', raw, basis_columns(nsamp), preferred_element_ty...  4.1 us
  transfers between devices with their start and end apart: 10, of which 4 were waited for; matrix products, arithmetic and copies ran while one was open for 5% of the time, Pallas kernels for 7%

profile of v1, /device:TPU:25, one launch (start us, length us, event | category | flops | bytes accessed | tf_op | source)
XLA Modules:
  0.0 125.8 jit_solution(5732052853138634255)
XLA Ops:
  0.0 0.8 convert_element_type.11
  0.8 3.7 %multiply_reduce_fusion = f32[128,4]{1,0:T(8,128)S(1)} fusion(bf16[128,4,3072]{2,1,0:T(4,128)(2,1)} %param.4), kind=kLoop, calls=%fused_computation | loop fusion | flops 4718080 | bytes 3147776 | tf_op jit(solution)/shard_map/reduce_sum | solution.py:146
  4.7 4.1 %fusion.14.spec_ref = bf16[4,128,256]{2,1,0:T(8,128)(2,1)} fusion(bf16[3072,256,1]{0,1,2:T(8,128)(2,1)} %constant.40, bf16[128,4,3072]{2,1,0:T(4,128)(2,1)S(1)} %copy-done, f32[128]{0:T(128)S(1)} %convert_element_type.11, f32[4,128]{1,0:T(4,128)S(1)} %bitcast.41, pred[4,128]{1,0:T(4,128)(4,1)S(1)} %broadcast_compare_fusion), kind=kOutput, calls=%fused_computation.7 | convolution fusion | flops 805830656 | bytes 4983808 | tf_op jit(solution)/shard_map/csn,nv->csv/dot_general | solution.py:148
  8.8 2.0 %pack.1 = bf16[4,272,128]{2,1,0:T(8,128)(2,1)} custom-call(s32[4]{0:T(128)} %use_ref.1, bf16[4,128,256]{2,1,0:T(8,128)(2,1)} %fusion.14.spec_ref), custom_call_target="tpu_custom_call" | custom-call | tf_op jit(solution)/shard_map/pack/pallas_call | solution.py:152
  10.8 13.0 %all_to_all.5 = bf16[4,272,128]{2,1,0:T(8,128)(2,1)S(1)} all-to-all(bf16[4,272,128]{2,1,0:T(8,128)(2,1)} %pack.1), channel_id=1, replica_groups=mesh['chan'=64,'h'=2,'q'=4] {'q'}, dimensions={0} | all-to-all | bytes 557056 | tf_op jit(solution)/shard_map/all_to_all | solution.py:161
  23.8 0.7 slice_bitcast_fusion.8
  24.5 8.8 %collective-permute-start.5 = (bf16[4,128,128]{2,1,0:T(8,128)(2,1)S(1)}, bf16[4,128,128]{2,1,0:T(8,128)(2,1)S(1)}, u32[]{:S(2)}, u32[]{:S(2)}) collective-permute-start(bf16[4,128,128]{2,1,0:T(8,128)(2,1)S(1)} %get-tuple-element.15.near_ref), channel_id=1, source_target_pairs={{0,4},{1,5},{2,6},{3,7},{4,0},{5,1},{6,2},{7,3},{8,12},{9,13},{10,... | collective-permute-start | bytes 393224 | tf_op jit(solution)/shard_map/ppermute | solution.py:171
  33.4 1.9 %collective-permute-start = (bf16[4,144,128]{2,1,0:T(8,128)(2,1)S(1)}, bf16[4,144,128]{2,1,0:T(8,128)(2,1)S(1)}, u32[]{:S(2)}, u32[]{:S(2)}) collective-permute-start(bf16[4,144,128]{2,1,0:T(8,128)(2,1)S(1)} %slice.59), channel_id=1, source_target_pairs={{0,4},{1,5},{2,6},{3,7},{4,0},{5,1},{6,2},{7,3},{8,12},{9,13},{10,... | collective-permute-start | bytes 442376 | tf_op jit(solution)/shard_map/ppermute | solution.py:171
  36.5 18.3 %collective-permute-done.5.far_ref = bf16[4,128,128]{2,1,0:T(8,128)(2,1)S(1)} collective-permute-done((bf16[4,128,128]{2,1,0:T(8,128)(2,1)S(1)}, bf16[4,128,128]{2,1,0:T(8,128)(2,1)S(1)}, u32[]{:S(2)}, u32[]{:S(2)}) %collective-permute-start.5) | collective-permute-done | bytes 131104 | tf_op jit(solution)/shard_map/ppermute | solution.py:171
  54.8 3.3 %collective-permute-start.6 = (bf16[2,4,128,128]{3,2,1,0:T(8,128)(2,1)S(1)}, bf16[2,4,128,128]{3,2,1,0:T(8,128)(2,1)S(1)}, u32[]{:S(2)}, u32[]{:S(2)}) collective-permute-start(bf16[2,4,128,128]{3,2,1,0:T(8,128)(2,1)S(1)} %pad_maximum_fusion.1), channel_id=1, source_target_pairs={{8,0},{9,1},{10,2},{11,3},{12,4},{13,5},{14,6},{15,7},{16,12},{17,... | collective-permute-start | bytes 786440 | tf_op jit(solution)/shard_map/ppermute | solution.py:178
  58.9 7.5 %collective-permute-start.1 = (bf16[2,4,128,128]{3,2,1,0:T(8,128)(2,1)S(1)}, bf16[2,4,128,128]{3,2,1,0:T(8,128)(2,1)S(1)}, u32[]{:S(2)}, u32[]{:S(2)}) collective-permute-start(bf16[2,4,128,128]{3,2,1,0:T(8,128)(2,1)S(1)} %pad_maximum_fusion), channel_id=1, source_target_pairs={{8,0},{9,1},{10,2},{11,3},{12,4},{13,5},{14,6},{15,7},{16,12},{17,... | collective-permute-start | bytes 786440 | tf_op jit(solution)/shard_map/ppermute | solution.py:178
  68.1 4.4 %stack.43 = bf16[4,512,128]{2,1,0:T(8,128)(2,1)} custom-call(s32[3]{0:T(128)} %pad_add_fusion.par_ref, bf16[4,128,128]{2,1,0:T(8,128)(2,1)} %copy-done.1, bf16[4,128,128]{2,1,0:T(8,128)(2,1)} %copy-done.2, bf16[2,4,128,128]{3,2,1,0:T(8,128)(2,1)} %copy-done.4, bf16[4,16,128]{2,1,0:T(8,128)(2,1)} %slice.61.nflag_ref, bf16[4,16,128]{2,1,0:T(8,128)(2,1)} %slice.62.fflag_ref), custom_call_target="tpu_custom_call" | custom-call | flops 268435456 | bytes 1048576 | tf_op jit(solution)/shard_map/stack/pallas_call | solution.py:179
  72.5 1.8 %slice_bitcast_fusion = (bf16[512,128]{1,0:T(8,128)(2,1)S(1)}, bf16[512,128]{1,0:T(8,128)(2,1)S(1)}, bf16[512,128]{1,0:T(8,128)(2,1)S(1)}, bf16[512,128]{1,0:T(8,128)(2,1)}) fusion(bf16[4,512,128]{2,1,0:T(8,128)(2,1)} %stack.43), kind=kLoop, calls=%fused_computation.10 | loop fusion | bytes 1048576 | tf_op jit(solution)/shard_map/squeeze | solution.py:191
  74.3 21.5 %collective-permute-start.9 = (bf16[512,128]{1,0:T(8,128)(2,1)S(1)}, bf16[512,128]{1,0:T(8,128)(2,1)S(1)}, u32[]{:S(2)}, u32[]{:S(2)}) collective-permute-start(bf16[512,128]{1,0:T(8,128)(2,1)S(1)} %get-tuple-element.5), channel_id=1, source_target_pairs={{0,3},{1,2},{2,1},{3,0},{4,7},{5,6},{6,5},{7,4},{8,11},{9,10},{10,... | collective-permute-start | bytes 393224 | tf_op jit(solution)/shard_map/ppermute | solution.py:191
  95.9 1.9 %collective-permute-start.8 = (bf16[512,128]{1,0:T(8,128)(2,1)S(1)}, bf16[512,128]{1,0:T(8,128)(2,1)S(1)}, u32[]{:S(2)}, u32[]{:S(2)}) collective-permute-start(bf16[512,128]{1,0:T(8,128)(2,1)S(1)} %get-tuple-element.6), channel_id=1, source_target_pairs={{0,2},{1,3},{2,0},{3,1},{4,6},{5,7},{6,4},{7,5},{8,10},{9,11},{10,... | collective-permute-start | bytes 393224 | tf_op jit(solution)/shard_map/ppermute | solution.py:191
  97.8 2.2 %collective-permute-start.7 = (bf16[512,128]{1,0:T(8,128)(2,1)S(1)}, bf16[512,128]{1,0:T(8,128)(2,1)S(1)}, u32[]{:S(2)}, u32[]{:S(2)}) collective-permute-start(bf16[512,128]{1,0:T(8,128)(2,1)S(1)} %get-tuple-element.7), channel_id=1, source_target_pairs={{0,1},{1,0},{2,3},{3,2},{4,5},{5,4},{6,7},{7,6},{8,9},{9,8},{10,11... | collective-permute-start | bytes 393224 | tf_op jit(solution)/shard_map/ppermute | solution.py:191
  100.7 4.4 %stack.42 = bf16[4,512,128]{2,1,0:T(8,128)(2,1)} custom-call(s32[3]{0:T(128)} %pad_add_fusion.par_ref, bf16[4,128,128]{2,1,0:T(8,128)(2,1)} %get-tuple-element.16.near_ref, bf16[4,128,128]{2,1,0:T(8,128)(2,1)} %get-tuple-element.18.far_ref, bf16[2,4,128,128]{3,2,1,0:T(8,128)(2,1)} %copy-done.3, bf16[4,16,128]{2,1,0:T(8,128)(2,1)} %slice.61.nflag_ref, ...), custom_call_target="tpu_custom_call" | custom-call | flops 268435456 | bytes 1048576 | tf_op jit(solution)/shard_map/stack/pallas_call | solution.py:179
  105.1 1.8 %slice_bitcast_fusion.4 = (bf16[512,128]{1,0:T(8,128)(2,1)S(1)}, bf16[512,128]{1,0:T(8,128)(2,1)S(1)}, bf16[512,128]{1,0:T(8,128)(2,1)S(1)}, bf16[512,128]{1,0:T(8,128)(2,1)}) fusion(bf16[4,512,128]{2,1,0:T(8,128)(2,1)} %stack.42), kind=kLoop, calls=%fused_computation.14 | loop fusion | bytes 1048576 | tf_op jit(solution)/shard_map/squeeze | solution.py:191
  106.9 5.2 %collective-permute-start.4 = (bf16[512,128]{1,0:T(8,128)(2,1)S(1)}, bf16[512,128]{1,0:T(8,128)(2,1)S(1)}, u32[]{:S(2)}, u32[]{:S(2)}) collective-permute-start(bf16[512,128]{1,0:T(8,128)(2,1)S(1)} %get-tuple-element.9), channel_id=1, source_target_pairs={{0,3},{1,2},{2,1},{3,0},{4,7},{5,6},{6,5},{7,4},{8,11},{9,10},{10,... | collective-permute-start | bytes 393224 | tf_op jit(solution)/shard_map/ppermute | solution.py:191
  112.0 1.9 %collective-permute-start.3 = (bf16[512,128]{1,0:T(8,128)(2,1)S(1)}, bf16[512,128]{1,0:T(8,128)(2,1)S(1)}, u32[]{:S(2)}, u32[]{:S(2)}) collective-permute-start(bf16[512,128]{1,0:T(8,128)(2,1)S(1)} %get-tuple-element.10), channel_id=1, source_target_pairs={{0,2},{1,3},{2,0},{3,1},{4,6},{5,7},{6,4},{7,5},{8,10},{9,11},{10,... | collective-permute-start | bytes 393224 | tf_op jit(solution)/shard_map/ppermute | solution.py:191
  114.0 2.2 %collective-permute-start.2 = (bf16[512,128]{1,0:T(8,128)(2,1)S(1)}, bf16[512,128]{1,0:T(8,128)(2,1)S(1)}, u32[]{:S(2)}, u32[]{:S(2)}) collective-permute-start(bf16[512,128]{1,0:T(8,128)(2,1)S(1)} %get-tuple-element.11), channel_id=1, source_target_pairs={{0,1},{1,0},{2,3},{3,2},{4,5},{5,4},{6,7},{7,6},{8,9},{9,8},{10,11... | collective-permute-start | bytes 393224 | tf_op jit(solution)/shard_map/ppermute | solution.py:191
  116.2 4.3 %collective-permute-done.3.refs_2_ = bf16[512,128]{1,0:T(8,128)(2,1)S(1)} collective-permute-done((bf16[512,128]{1,0:T(8,128)(2,1)S(1)}, bf16[512,128]{1,0:T(8,128)(2,1)S(1)}, u32[]{:S(2)}, u32[]{:S(2)}) %collective-permute-start.3) | collective-permute-done | bytes 131104 | tf_op jit(solution)/shard_map/ppermute | solution.py:191
  120.5 0.9 collective-permute-done.2.refs_1_
  122.1 3.7 %turn.1 = bf16[16,128,256]{2,1,0:T(8,128)(2,1)} custom-call(s32[3]{0:T(128)} %pad_add_fusion.par_ref, bf16[512,128]{1,0:T(8,128)(2,1)} %get-tuple-element.12.refs_0_, bf16[512,128]{1,0:T(8,128)(2,1)} %copy-done.10, bf16[512,128]{1,0:T(8,128)(2,1)} %copy-done.9, bf16[512,128]{1,0:T(8,128)(2,1)} %copy-done.8, bf16[512,128]{1,0:T(8,128)(2,1)} %get-tuple-element.8.refs_4_, ...), custom_call_target="tpu_custom_call" | custom-call | tf_op jit(solution)/shard_map/turn/pallas_call | solution.py:195
  (39 shorter events, 5.2 us)
Async XLA Ops:
  0.0 4.7 %copy-start = (bf16[128,4,3072]{2,1,0:T(4,128)(2,1)S(1)}, bf16[128,4,3072]{2,1,0:T(4,128)(2,1)}, u32[]{:S(2)}) copy-start(bf16[128,4,3072]{2,1,0:T(4,128)(2,1)} %param.4) | copy-start | bytes 9437188
  24.5 42.9 %copy-start.1 = (bf16[4,128,128]{2,1,0:T(8,128)(2,1)}, bf16[4,128,128]{2,1,0:T(8,128)(2,1)S(1)}, u32[]{:S(2)}) copy-start(bf16[4,128,128]{2,1,0:T(8,128)(2,1)S(1)} %get-tuple-element.15.near_ref) | copy-start | bytes 393220
  24.5 30.3 %collective-permute-start.5 = (bf16[4,128,128]{2,1,0:T(8,128)(2,1)S(1)}, bf16[4,128,128]{2,1,0:T(8,128)(2,1)S(1)}, u32[]{:S(2)}, u32[]{:S(2)}) collective-permute-start(bf16[4,128,128]{2,1,0:T(8,128)(2,1)S(1)} %get-tuple-element.15.near_ref), channel_id=1, source_target_pairs={{0,4},{1,5},{2,6},{3,7},{4,0},{5,1},{6,2},{7,3},{8,12},{9,13},{10,... | collective-permute-start | bytes 393224 | tf_op jit(solution)/shard_map/ppermute | solution.py:171
  33.4 24.8 %collective-permute-start = (bf16[4,144,128]{2,1,0:T(8,128)(2,1)S(1)}, bf16[4,144,128]{2,1,0:T(8,128)(2,1)S(1)}, u32[]{:S(2)}, u32[]{:S(2)}) collective-permute-start(bf16[4,144,128]{2,1,0:T(8,128)(2,1)S(1)} %slice.59), channel_id=1, source_target_pairs={{0,4},{1,5},{2,6},{3,7},{4,0},{5,1},{6,2},{7,3},{8,12},{9,13},{10,... | collective-permute-start | bytes 442376 | tf_op jit(solution)/shard_map/ppermute | solution.py:171
  54.8 12.6 %copy-start.2 = (bf16[4,128,128]{2,1,0:T(8,128)(2,1)}, bf16[4,128,128]{2,1,0:T(8,128)(2,1)S(1)}, u32[]{:S(2)}) copy-start(bf16[4,128,128]{2,1,0:T(8,128)(2,1)S(1)} %collective-permute-done.5.far_ref) | copy-start | bytes 393220
  54.8 12.6 %collective-permute-start.6 = (bf16[2,4,128,128]{3,2,1,0:T(8,128)(2,1)S(1)}, bf16[2,4,128,128]{3,2,1,0:T(8,128)(2,1)S(1)}, u32[]{:S(2)}, u32[]{:S(2)}) collective-permute-start(bf16[2,4,128,128]{3,2,1,0:T(8,128)(2,1)S(1)} %pad_maximum_fusion.1), channel_id=1, source_target_pairs={{8,0},{9,1},{10,2},{11,3},{12,4},{13,5},{14,6},{15,7},{16,12},{17,... | collective-permute-start | bytes 786440 | tf_op jit(solution)/shard_map/ppermute | solution.py:178
  58.9 41.1 %collective-permute-start.1 = (bf16[2,4,128,128]{3,2,1,0:T(8,128)(2,1)S(1)}, bf16[2,4,128,128]{3,2,1,0:T(8,128)(2,1)S(1)}, u32[]{:S(2)}, u32[]{:S(2)}) collective-permute-start(bf16[2,4,128,128]{3,2,1,0:T(8,128)(2,1)S(1)} %pad_maximum_fusion), channel_id=1, source_target_pairs={{8,0},{9,1},{10,2},{11,3},{12,4},{13,5},{14,6},{15,7},{16,12},{17,... | collective-permute-start | bytes 786440 | tf_op jit(solution)/shard_map/ppermute | solution.py:178
  67.4 0.7 copy-start.4
  74.3 39.6 %collective-permute-start.9 = (bf16[512,128]{1,0:T(8,128)(2,1)S(1)}, bf16[512,128]{1,0:T(8,128)(2,1)S(1)}, u32[]{:S(2)}, u32[]{:S(2)}) collective-permute-start(bf16[512,128]{1,0:T(8,128)(2,1)S(1)} %get-tuple-element.5), channel_id=1, source_target_pairs={{0,3},{1,2},{2,1},{3,0},{4,7},{5,6},{6,5},{7,4},{8,11},{9,10},{10,... | collective-permute-start | bytes 393224 | tf_op jit(solution)/shard_map/ppermute | solution.py:191
  95.9 20.3 %collective-permute-start.8 = (bf16[512,128]{1,0:T(8,128)(2,1)S(1)}, bf16[512,128]{1,0:T(8,128)(2,1)S(1)}, u32[]{:S(2)}, u32[]{:S(2)}) collective-permute-start(bf16[512,128]{1,0:T(8,128)(2,1)S(1)} %get-tuple-element.6), channel_id=1, source_target_pairs={{0,2},{1,3},{2,0},{3,1},{4,6},{5,7},{6,4},{7,5},{8,10},{9,11},{10,... | collective-permute-start | bytes 393224 | tf_op jit(solution)/shard_map/ppermute | solution.py:191
  97.8 18.4 %collective-permute-start.7 = (bf16[512,128]{1,0:T(8,128)(2,1)S(1)}, bf16[512,128]{1,0:T(8,128)(2,1)S(1)}, u32[]{:S(2)}, u32[]{:S(2)}) collective-permute-start(bf16[512,128]{1,0:T(8,128)(2,1)S(1)} %get-tuple-element.7), channel_id=1, source_target_pairs={{0,1},{1,0},{2,3},{3,2},{4,5},{5,4},{6,7},{7,6},{8,9},{9,8},{10,11... | collective-permute-start | bytes 393224 | tf_op jit(solution)/shard_map/ppermute | solution.py:191
  100.0 0.7 copy-start.3
  106.9 9.4 %collective-permute-start.4 = (bf16[512,128]{1,0:T(8,128)(2,1)S(1)}, bf16[512,128]{1,0:T(8,128)(2,1)S(1)}, u32[]{:S(2)}, u32[]{:S(2)}) collective-permute-start(bf16[512,128]{1,0:T(8,128)(2,1)S(1)} %get-tuple-element.9), channel_id=1, source_target_pairs={{0,3},{1,2},{2,1},{3,0},{4,7},{5,6},{6,5},{7,4},{8,11},{9,10},{10,... | collective-permute-start | bytes 393224 | tf_op jit(solution)/shard_map/ppermute | solution.py:191
  112.0 8.5 %collective-permute-start.3 = (bf16[512,128]{1,0:T(8,128)(2,1)S(1)}, bf16[512,128]{1,0:T(8,128)(2,1)S(1)}, u32[]{:S(2)}, u32[]{:S(2)}) collective-permute-start(bf16[512,128]{1,0:T(8,128)(2,1)S(1)} %get-tuple-element.10), channel_id=1, source_target_pairs={{0,2},{1,3},{2,0},{3,1},{4,6},{5,7},{6,4},{7,5},{8,10},{9,11},{10,... | collective-permute-start | bytes 393224 | tf_op jit(solution)/shard_map/ppermute | solution.py:191
  114.0 7.5 %copy-start.5 = (bf16[512,128]{1,0:T(8,128)(2,1)}, bf16[512,128]{1,0:T(8,128)(2,1)S(1)}, u32[]{:S(2)}) copy-start(bf16[512,128]{1,0:T(8,128)(2,1)S(1)} %collective-permute-done.9.refs_7_) | copy-start | bytes 393220
  114.0 7.5 %collective-permute-start.2 = (bf16[512,128]{1,0:T(8,128)(2,1)S(1)}, bf16[512,128]{1,0:T(8,128)(2,1)S(1)}, u32[]{:S(2)}, u32[]{:S(2)}) collective-permute-start(bf16[512,128]{1,0:T(8,128)(2,1)S(1)} %get-tuple-element.11), channel_id=1, source_target_pairs={{0,1},{1,0},{2,3},{3,2},{4,5},{5,4},{6,7},{7,6},{8,9},{9,8},{10,11... | collective-permute-start | bytes 393224 | tf_op jit(solution)/shard_map/ppermute | solution.py:191
  116.2 5.2 %copy-start.6 = (bf16[512,128]{1,0:T(8,128)(2,1)}, bf16[512,128]{1,0:T(8,128)(2,1)S(1)}, u32[]{:S(2)}) copy-start(bf16[512,128]{1,0:T(8,128)(2,1)S(1)} %collective-permute-done.8.refs_6_) | copy-start | bytes 393220
  116.2 5.2 %copy-start.7 = (bf16[512,128]{1,0:T(8,128)(2,1)}, bf16[512,128]{1,0:T(8,128)(2,1)S(1)}, u32[]{:S(2)}) copy-start(bf16[512,128]{1,0:T(8,128)(2,1)S(1)} %collective-permute-done.7.refs_5_) | copy-start | bytes 393220
  116.2 5.2 %copy-start.8 = (bf16[512,128]{1,0:T(8,128)(2,1)}, bf16[512,128]{1,0:T(8,128)(2,1)S(1)}, u32[]{:S(2)}) copy-start(bf16[512,128]{1,0:T(8,128)(2,1)S(1)} %collective-permute-done.4.refs_3_) | copy-start | bytes 393220
  120.5 0.9 copy-start.9
  121.4 0.7 copy-start.10

commit v2 on v1

v2 whole, which is shorter than its diff:
```python
import functools
import math

import jax
import jax.numpy as jnp
import ml_dtypes
import numpy as np
from jax import lax
from jax.experimental import pallas as pl
from jax.experimental.pallas import tpu as pltpu
from jax.sharding import Mesh
from jax.sharding import PartitionSpec as P

BINS = 128
OFFS = 128
GROUP = 16
QUADS = 4
BATCHES = 2
FLAG_ROWS = 16
N_STEPS = 2
F32 = jnp.float32
BF16 = jnp.bfloat16
VMEM = pl.BlockSpec(memory_space=pltpu.VMEM)
SMEM = pl.BlockSpec(memory_space=pltpu.SMEM)
BIG = pltpu.CompilerParams(vmem_limit_bytes=60 * 2**20)


def basis_columns(nsamp):
    times = np.arange(nsamp, dtype=np.int32)[:, None]
    freqs = np.arange(1, BINS + 1, dtype=np.int32)[None, :]
    phase = (times * freqs % nsamp).astype(np.float32) * np.float32(2.0 * math.pi / nsamp)
    scale = np.float32(1.0 / math.sqrt(nsamp))
    both = np.stack([np.cos(phase) * scale, -np.sin(phase) * scale], axis=-1)
    return both.reshape(nsamp, 2 * BINS).astype(ml_dtypes.bfloat16)


def dot_nt(left, right):
    return lax.dot_general(left, right, (((1,), (1,)), ((), ())), preferred_element_type=F32)


def unit(size):
    rows = lax.broadcasted_iota(jnp.int32, (size, size), 0)
    return (rows == lax.broadcasted_iota(jnp.int32, (size, size), 1)).astype(F32).astype(BF16)


def spectrum_kernel(nsamp, use_ref, alive_ref, raw_ref, basis_ref, *refs):
    outs, (spec, square, turned) = refs[:-3], refs[-3:]
    channels, segs, part = raw_ref.shape
    step = pl.program_id(0)
    flat = raw_ref[...].reshape(channels * segs, part)
    signal = flat.astype(F32)
    signal = signal * signal
    squares = signal[:, :128]
    for col in range(128, part, 128):
        squares += signal[:, col : col + 128]
    product = jnp.dot(flat, basis_ref[...], preferred_element_type=F32)

    @pl.when(step == 0)
    def _():
        for col in range(2):
            spec[col] = product[:, 128 * col : 128 * col + 128]
        square[...] = squares

    @pl.when(step > 0)
    def _():
        for col in range(2):
            spec[col] += product[:, 128 * col : 128 * col + 128]
        square[...] += squares

    @pl.when(step == pl.num_programs(0) - 1)
    def _():
        meansq = jnp.sum(square[...], axis=1, keepdims=True) * (1.0 / nsamp)
        scale = lax.rsqrt(meansq + 1e-06)
        for col in range(2):
            spec[col] = jnp.where(scale > 0, spec[col] * scale, 0.0)
        width = 2 * 128
        alive = alive_ref[...].astype(F32)
        for seg in range(segs):
            rows = [spec[col, pl.ds(seg, channels, stride=segs), :].astype(BF16) for col in range(2)]
            rows = jnp.concatenate(rows, axis=1)
            turned[pl.ds(seg, width, stride=segs), :] = dot_nt(unit(width), rows) * alive
        seg_of_row = lax.broadcasted_iota(jnp.int32, (FLAG_ROWS, channels), 0) % segs
        flags = jnp.zeros((FLAG_ROWS, channels), F32)
        for seg in range(segs):
            flags = jnp.where(seg_of_row == seg, use_ref[seg].astype(F32), flags)
        flags = flags.astype(BF16)
        depth = width * segs // (QUADS * BATCHES)
        for quad in range(QUADS):
            for batch in range(BATCHES):
                start = (quad * BATCHES + batch) * depth
                value = turned[start : start + depth, :].astype(BF16)
                for half in range(2):
                    dest = half * QUADS + quad
                    if batch == 0:
                        outs[0][dest, :FLAG_ROWS, :] = flags
                        outs[0][dest, FLAG_ROWS:, :] = value
                    else:
                        outs[batch][dest] = value


def stack_kernel(total_segs, first, par_ref, own_ref, halo_ref, flag_ref, *refs):
    outs, scratch = refs[:QUADS], refs[QUADS]
    half, quad = par_ref[0], par_ref[1]
    srcs, _, width = own_ref.shape
    depth = GROUP * 8

    def inverse(ref):
        value = ref[:, first : first + depth, :].astype(F32)
        total = jnp.sum(value * value, axis=(0, 1))[None, :]
        return lax.rsqrt(total * (1.0 / (GROUP * total_segs)) + 1e-06)

    own_scale = inverse(own_ref)
    col_scale = jnp.concatenate([own_scale, inverse(halo_ref)], axis=1) * (1.0 / total_segs)
    pick = lax.broadcasted_iota(jnp.int32, (64, width), 1) == (
        64 * half + 63 - lax.broadcasted_iota(jnp.int32, (64, width), 0)
    )
    row_scale = jnp.sum(jnp.where(pick, own_scale, 0.0), axis=1, keepdims=True)
    scale = row_scale * col_scale
    pick = pick.astype(F32).astype(BF16)

    row = lax.broadcasted_iota(jnp.int32, (depth, depth), 0)
    col = lax.broadcasted_iota(jnp.int32, (depth, depth), 1)
    flags = flag_ref[:, :FLAG_ROWS, :].reshape(depth, width).astype(F32)
    place = []
    for bin_ in range(2):
        keep = (col // 8) % 2 == bin_
        sign = jnp.where((col // 4) % 2 == 0, 1.0, -1.0)
        place.append(jnp.where(keep & (row == col), flags, 0.0))
        place.append(jnp.where(keep & (row == (col ^ 4)), flags * sign, 0.0))
    place = jnp.concatenate(place, axis=1).astype(BF16)

    owns = []
    for pair in range(GROUP // 2):
        rows = slice(first + 16 * pair, first + 16 * pair + 16)
        owns.append(own_ref[:, rows, :].reshape(depth, width))
    turned = dot_nt(pick, jnp.concatenate(owns, axis=0)).astype(BF16)
    turned = jnp.concatenate([turned[:, depth * k : depth * k + depth] for k in range(GROUP // 2)], axis=0)
    lefts = jnp.dot(turned, place, preferred_element_type=F32).astype(BF16)

    def fill(which):
        for pair in range(GROUP // 2):
            rows = slice(first + 16 * pair, first + 16 * pair + 16)
            behind = halo_ref[:, rows, :].reshape(depth, width)
            left = lefts[64 * pair : 64 * pair + 64]
            left = jnp.concatenate([left[:, 128 * k : 128 * k + 128] for k in range(4)], axis=0)
            right = jnp.concatenate([owns[pair], behind], axis=1)
            both = jnp.dot(left, right, preferred_element_type=F32)
            for bin_ in range(2):
                for part in range(2):
                    k = 2 * bin_ + part
                    block = both[64 * k : 64 * k + 64] * scale
                    block = pltpu.roll(block, 193 - 64 * which, 1, stride=1, stride_axis=0)
                    scratch[pl.ds(part * 16 + 2 * pair + bin_, 64, stride=32), :] = block[:, :OFFS]

    for which in range(2):
        pl.when(half == which)(functools.partial(fill, which))
    for slot in range(QUADS):
        start = pl.multiple_of((3 - (quad ^ slot)) * 512, 512)
        outs[slot][...] = scratch[pl.ds(start, 512), :].astype(BF16)


def turn_kernel(par_ref, *refs):
    parts, out_ref, scratch = refs[:-2], refs[-2], refs[-1]
    quad = par_ref[1]
    count = out_ref.shape[0]
    for index, ref in enumerate(parts):
        batch, slot = index // QUADS, index % QUADS
        group = (quad ^ slot) * BATCHES + batch
        for row in range(count):
            for part in range(2):
                start = pl.multiple_of(part * 128 + GROUP * group, GROUP)
                begin = (2 * row + part) * GROUP
                scratch[count - 1 - row, pl.ds(start, GROUP), :] = ref[begin : begin + GROUP, :]
    eye = unit(OFFS)
    for row in range(count):
        out_ref[row] = dot_nt(eye, scratch[row]).astype(BF16)


def spectra(raw, alive, use):
    channels, segs, nsamp = raw.shape
    depth = 2 * BINS * segs // (QUADS * BATCHES)
    part = nsamp // N_STEPS
    return pl.pallas_call(
        functools.partial(spectrum_kernel, nsamp),
        out_shape=[
            jax.ShapeDtypeStruct((2 * QUADS, depth + (FLAG_ROWS if batch == 0 else 0), channels), BF16)
            for batch in range(BATCHES)
        ],
        grid=(N_STEPS,),
        in_specs=[
            SMEM,
            VMEM,
            pl.BlockSpec((channels, segs, part), lambda step: (0, 0, step)),
            pl.BlockSpec((part, 2 * BINS), lambda step: (step, 0)),
        ],
        out_specs=[VMEM] * BATCHES,
        scratch_shapes=[
            pltpu.VMEM((2, channels * segs, BINS), F32),
            pltpu.VMEM((channels * segs, 128), F32),
            pltpu.VMEM((2 * BINS * segs, channels), F32),
        ],
        compiler_params=BIG,
        name="spectra",
    )(use, alive[None, :], raw, basis_columns(nsamp))


def stack_pairs(par, own, halo, flags, total_segs, first):
    return pl.pallas_call(
        functools.partial(stack_kernel, total_segs, first),
        out_shape=[jax.ShapeDtypeStruct((512, OFFS), BF16)] * QUADS,
        in_specs=[SMEM] + [VMEM] * 3,
        out_specs=[VMEM] * QUADS,
        scratch_shapes=[pltpu.VMEM((512 * QUADS, OFFS), F32)],
        cost_estimate=pl.CostEstimate(flops=2 * 8 * 256 * 256 * 256, bytes_accessed=2**20, transcendentals=0),
        name="stack",
    )(par, own, halo, flags)


def turn_pieces(par, pieces, sub):
    steps = 2
    return pl.pallas_call(
        turn_kernel,
        out_shape=jax.ShapeDtypeStruct((sub, OFFS, 2 * BINS), BF16),
        grid=(steps,),
        in_specs=[SMEM] + [pl.BlockSpec((512 // steps, OFFS), lambda step: (steps - 1 - step, 0))] * len(pieces),
        out_specs=pl.BlockSpec((sub // steps, OFFS, 2 * BINS), lambda step: (step, 0, 0)),
        scratch_shapes=[pltpu.VMEM((sub // steps, 2 * BINS, OFFS), BF16)],
        name="turn",
    )(par, *pieces)


def shards(raw, alive, use):
    channels, seg_local, _ = raw.shape
    chans = lax.axis_size("chan")
    total_segs = seg_local * lax.axis_size("h") * lax.axis_size("q")
    axes = ("chan", "h", "q")
    par = jnp.stack([lax.axis_index("h"), lax.axis_index("q")]).astype(jnp.int32)

    def index(chan, half, quad):
        return (chan * 2 + half) * QUADS + quad

    places = [(c, h, q) for c in range(chans) for h in range(2) for q in range(QUADS)]
    behind = [(index(c, h, q), index(c - 1, h if c % 2 else 1 - h, q)) for c, h, q in places if c > 0]

    owns = [lax.all_to_all(message, ("h", "q"), 0, 0, tiled=True) for message in spectra(raw, alive, use)]
    halos = [lax.ppermute(own, axes, behind) for own in owns]
    pieces = []
    for batch, (own, halo) in enumerate(zip(owns, halos)):
        first = FLAG_ROWS if batch == 0 else 0
        stacked = stack_pairs(par, own, halo, owns[0], total_segs, first)
        part = [stacked[0]] + [None] * (QUADS - 1)
        for slot in (2, 3, 1):
            pairs = [(index(c, h, q), index(c, h, q ^ slot)) for c, h, q in places]
            part[slot] = lax.ppermute(stacked[slot], axes, pairs)
        pieces += part
    return turn_pieces(par, pieces, channels // (2 * QUADS))


def solution(mesh):
    chans, groups = mesh.devices.shape
    fine = Mesh(mesh.devices.reshape(chans, 2, groups // 2), ("chan", "h", "q"))
    in_specs = (P("chan", ("h", "q"), None), P("chan"), P(("h", "q")))
    out_specs = P(("chan", "h", "q"), None, None)
    return jax.shard_map(shards, mesh=fine, in_specs=in_specs, out_specs=out_specs, check_vma=False)
```

time: 127 us -> 103 us (0.81)
  the two profiles are of different devices: /device:TPU:25 before, /device:TPU:32 now
where the time goes in v2:
time: 103 us; the launch traced here: 102 us
  starting transfers between devices  29.8 us (29%)
  blocking collectives  28.9 us (28%)
  waiting for transfers between devices  26.1 us (25%)
  Pallas kernels  14.8 us (14%)
  local copies, waits for them, and re-layouts  2.05 us (2%)
    all_to_all x1, blocking collectives, shards(): lax.all_to_all(message, ('h', 'q'), 0, 0, tiled=True)  28.9 us
    ppermute x6, starting transfers between devices, shards(): part[slot] = lax.ppermute(stacked[slot], axes, pairs)  21.8 us
    all_to_all x1, waiting for transfers between devices, shards(): lax.all_to_all(message, ('h', 'q'), 0, 0, tiled=True)  15.8 us
    ppermute x6, waiting for transfers between devices, shards(): part[slot] = lax.ppermute(stacked[slot], axes, pairs)  10.3 us
    pallas_call x2, Pallas kernels, stack_pairs(): pl.pallas_call(functools.partial(stack_kernel, total_segs, first), out_sh...  7.27 us
    all_to_all x1, starting transfers between devices, shards(): lax.all_to_all(message, ('h', 'q'), 0, 0, tiled=True)  5.47 us
    pallas_call x1, Pallas kernels, spectra(): pl.pallas_call(functools.partial(spectrum_kernel, nsamp), out_shape=[jax....  4.82 us
    pallas_call x1, Pallas kernels, turn_pieces(): pl.pallas_call(turn_kernel, out_shape=jax.ShapeDtypeStruct((sub, OFFS, 2...  2.68 us
  transfers between devices with their start and end apart: 9, of which 3 were waited for; matrix products, arithmetic and copies ran while one was open for 1% of the time, Pallas kernels for 7%

profile of v2, /device:TPU:32, one launch (start us, length us, event | category | flops | bytes accessed | tf_op | source)
XLA Modules:
  0.0 102.5 jit_solution(11952083659503748085)
XLA Ops:
  0.0 4.8 %spectra.1 = (bf16[8,144,128]{2,1,0:T(8,128)(2,1)}, bf16[8,128,128]{2,1,0:T(8,128)(2,1)}) custom-call(s32[4]{0:T(128)} %use_ref.1, s32[1,128]{1,0:T(1,128)} %bitcast.3, bf16[128,4,3072]{2,1,0:T(4,128)(2,1)} %raw_ref.1, bf16[3072,256]{1,0:T(8,128)(2,1)} %constant.11.clone.basis_ref), custom_call_target="tpu_custom_call" | custom-call | tf_op jit(solution)/shard_map/spectra/pallas_call | solution.py:183
  4.8 28.9 %all_to_all.10.own_ref = bf16[8,128,128]{2,1,0:T(8,128)(2,1)S(1)} all-to-all(bf16[8,128,128]{2,1,0:T(8,128)(2,1)} %get-tuple-element.20), channel_id=1, replica_groups=mesh['chan'=64,'h'=2,'q'=4] {'h','q'}, dimensions={0} | all-to-all | bytes 524288 | tf_op jit(solution)/shard_map/all_to_all | solution.py:245
  33.7 5.5 %all-to-all-start = ((bf16[8,144,128]{2,1,0:T(8,128)(2,1)}), bf16[8,144,128]{2,1,0:T(8,128)(2,1)S(1)}, u32[]{:S(2)}, u32[]{:S(2)}) async-start(bf16[8,144,128]{2,1,0:T(8,128)(2,1)} %get-tuple-element.15), calls=%async_computation | async-start | bytes 589824 | tf_op jit(solution)/shard_map/all_to_all | solution.py:245
  39.2 1.3 %collective-permute-start.4 = (bf16[8,128,128]{2,1,0:T(8,128)(2,1)S(1)}, bf16[8,128,128]{2,1,0:T(8,128)(2,1)S(1)}, u32[]{:S(2)}, u32[]{:S(2)}) collective-permute-start(bf16[8,128,128]{2,1,0:T(8,128)(2,1)S(1)} %all_to_all.10.own_ref), channel_id=1, source_target_pairs={{8,0},{9,1},{10,2},{11,3},{12,4},{13,5},{14,6},{15,7},{16,12},{17,... | collective-permute-start | bytes 786440 | tf_op jit(solution)/shard_map/ppermute | solution.py:246
  40.5 15.8 %all-to-all-done.own_ref.flag_ref = bf16[8,144,128]{2,1,0:T(8,128)(2,1)S(1)} async-done(((bf16[8,144,128]{2,1,0:T(8,128)(2,1)}), bf16[8,144,128]{2,1,0:T(8,128)(2,1)S(1)}, u32[]{:S(2)}, u32[]{:S(2)}) %all-to-all-start) | async-done | bytes 294944 | tf_op jit(solution)/shard_map/all_to_all | solution.py:245
  56.3 1.3 %collective-permute-start = (bf16[8,144,128]{2,1,0:T(8,128)(2,1)S(1)}, bf16[8,144,128]{2,1,0:T(8,128)(2,1)S(1)}, u32[]{:S(2)}, u32[]{:S(2)}) collective-permute-start(bf16[8,144,128]{2,1,0:T(8,128)(2,1)S(1)} %all-to-all-done.own_ref.flag_ref), channel_id=1, source_target_pairs={{8,0},{9,1},{10,2},{11,3},{12,4},{13,5},{14,6},{15,7},{16,12},{17,... | collective-permute-start | bytes 884744 | tf_op jit(solution)/shard_map/ppermute | solution.py:246
  57.6 0.6 pad_add_fusion.par_ref
  58.2 0.0 collective-permute-done.4.halo_ref
  58.3 0.7 copy-done.9
  58.9 3.6 %stack.15 = (bf16[512,128]{1,0:T(8,128)(2,1)}, bf16[512,128]{1,0:T(8,128)(2,1)}, bf16[512,128]{1,0:T(8,128)(2,1)}, bf16[512,128]{1,0:T(8,128)(2,1)}) custom-call(s32[2]{0:T(128)} %pad_add_fusion.par_ref, bf16[8,128,128]{2,1,0:T(8,128)(2,1)} %copy-done.1, bf16[8,128,128]{2,1,0:T(8,128)(2,1)} %copy-done.9, bf16[8,144,128]{2,1,0:T(8,128)(2,1)} %copy-done), custom_call_target="tpu_custom_call" | custom-call | flops 268435456 | bytes 1048576 | tf_op jit(solution)/shard_map/stack/pallas_call | solution.py:208
  62.6 6.4 %collective-permute-start.5 = (bf16[512,128]{1,0:T(8,128)(2,1)}, bf16[512,128]{1,0:T(8,128)(2,1)S(1)}, u32[]{:S(2)}, u32[]{:S(2)}) collective-permute-start(bf16[512,128]{1,0:T(8,128)(2,1)} %get-tuple-element.22), channel_id=1, source_target_pairs={{0,1},{1,0},{2,3},{3,2},{4,5},{5,4},{6,7},{7,6},{8,9},{9,8},{10,11... | collective-permute-start | bytes 393224 | tf_op jit(solution)/shard_map/ppermute | solution.py:254
  68.9 3.3 %collective-permute-start.6 = (bf16[512,128]{1,0:T(8,128)(2,1)}, bf16[512,128]{1,0:T(8,128)(2,1)S(1)}, u32[]{:S(2)}, u32[]{:S(2)}) collective-permute-start(bf16[512,128]{1,0:T(8,128)(2,1)} %get-tuple-element.23), channel_id=1, source_target_pairs={{0,2},{1,3},{2,0},{3,1},{4,6},{5,7},{6,4},{7,5},{8,10},{9,11},{10,... | collective-permute-start | bytes 393224 | tf_op jit(solution)/shard_map/ppermute | solution.py:254
  72.2 2.0 %collective-permute-start.7 = (bf16[512,128]{1,0:T(8,128)(2,1)}, bf16[512,128]{1,0:T(8,128)(2,1)S(1)}, u32[]{:S(2)}, u32[]{:S(2)}) collective-permute-start(bf16[512,128]{1,0:T(8,128)(2,1)} %get-tuple-element.24), channel_id=1, source_target_pairs={{0,3},{1,2},{2,1},{3,0},{4,7},{5,6},{6,5},{7,4},{8,11},{9,10},{10,... | collective-permute-start | bytes 393224 | tf_op jit(solution)/shard_map/ppermute | solution.py:254
  74.3 0.0 collective-permute-done.halo_ref
  74.3 0.7 copy-done.8
  75.0 3.7 %stack.14 = (bf16[512,128]{1,0:T(8,128)(2,1)}, bf16[512,128]{1,0:T(8,128)(2,1)}, bf16[512,128]{1,0:T(8,128)(2,1)}, bf16[512,128]{1,0:T(8,128)(2,1)}) custom-call(s32[2]{0:T(128)} %pad_add_fusion.par_ref, bf16[8,144,128]{2,1,0:T(8,128)(2,1)} %copy-done, bf16[8,144,128]{2,1,0:T(8,128)(2,1)} %copy-done.8, bf16[8,144,128]{2,1,0:T(8,128)(2,1)} %copy-done), custom_call_target="tpu_custom_call" | custom-call | flops 268435456 | bytes 1048576 | tf_op jit(solution)/shard_map/stack/pallas_call | solution.py:208
  78.6 4.8 %collective-permute-start.1 = (bf16[512,128]{1,0:T(8,128)(2,1)}, bf16[512,128]{1,0:T(8,128)(2,1)S(1)}, u32[]{:S(2)}, u32[]{:S(2)}) collective-permute-start(bf16[512,128]{1,0:T(8,128)(2,1)} %get-tuple-element.17), channel_id=1, source_target_pairs={{0,1},{1,0},{2,3},{3,2},{4,5},{5,4},{6,7},{7,6},{8,9},{9,8},{10,11... | collective-permute-start | bytes 393224 | tf_op jit(solution)/shard_map/ppermute | solution.py:254
  83.4 2.4 %collective-permute-start.2 = (bf16[512,128]{1,0:T(8,128)(2,1)}, bf16[512,128]{1,0:T(8,128)(2,1)S(1)}, u32[]{:S(2)}, u32[]{:S(2)}) collective-permute-start(bf16[512,128]{1,0:T(8,128)(2,1)} %get-tuple-element.18), channel_id=1, source_target_pairs={{0,2},{1,3},{2,0},{3,1},{4,6},{5,7},{6,4},{7,5},{8,10},{9,11},{10,... | collective-permute-start | bytes 393224 | tf_op jit(solution)/shard_map/ppermute | solution.py:254
  85.8 0.0 collective-permute-done.5.refs_5_
  85.8 2.9 %collective-permute-start.3 = (bf16[512,128]{1,0:T(8,128)(2,1)}, bf16[512,128]{1,0:T(8,128)(2,1)S(1)}, u32[]{:S(2)}, u32[]{:S(2)}) collective-permute-start(bf16[512,128]{1,0:T(8,128)(2,1)} %get-tuple-element.19), channel_id=1, source_target_pairs={{0,3},{1,2},{2,1},{3,0},{4,7},{5,6},{6,5},{7,4},{8,11},{9,10},{10,... | collective-permute-start | bytes 393224 | tf_op jit(solution)/shard_map/ppermute | solution.py:254
  88.8 6.6 %collective-permute-done.2.refs_2_ = bf16[512,128]{1,0:T(8,128)(2,1)S(1)} collective-permute-done((bf16[512,128]{1,0:T(8,128)(2,1)}, bf16[512,128]{1,0:T(8,128)(2,1)S(1)}, u32[]{:S(2)}, u32[]{:S(2)}) %collective-permute-start.2) | collective-permute-done | bytes 131104 | tf_op jit(solution)/shard_map/ppermute | solution.py:254
  95.4 3.7 %collective-permute-done.3.refs_3_ = bf16[512,128]{1,0:T(8,128)(2,1)S(1)} collective-permute-done((bf16[512,128]{1,0:T(8,128)(2,1)}, bf16[512,128]{1,0:T(8,128)(2,1)S(1)}, u32[]{:S(2)}, u32[]{:S(2)}) %collective-permute-start.3) | collective-permute-done | bytes 131104 | tf_op jit(solution)/shard_map/ppermute | solution.py:254
  99.2 0.6 copy-done.7
  99.8 2.7 %turn.1 = bf16[16,128,256]{2,1,0:T(8,128)(2,1)} custom-call(s32[2]{0:T(128)} %pad_add_fusion.par_ref, bf16[512,128]{1,0:T(8,128)(2,1)} %get-tuple-element.16.refs_0_, bf16[512,128]{1,0:T(8,128)(2,1)} %copy-done.5, bf16[512,128]{1,0:T(8,128)(2,1)} %copy-done.6, bf16[512,128]{1,0:T(8,128)(2,1)} %copy-done.7, bf16[512,128]{1,0:T(8,128)(2,1)} %get-tuple-element.21.refs_4_, ...), custom_call_target="tpu_custom_call" | custom-call | tf_op jit(solution)/shard_map/turn/pallas_call | solution.py:221
  (20 shorter events, 0.0 us)
Async XLA Ops:
  33.7 24.5 %copy-start.1 = (bf16[8,128,128]{2,1,0:T(8,128)(2,1)}, bf16[8,128,128]{2,1,0:T(8,128)(2,1)S(1)}, u32[]{:S(2)}) copy-start(bf16[8,128,128]{2,1,0:T(8,128)(2,1)S(1)} %all_to_all.10.own_ref) | copy-start | bytes 786436
  33.7 22.6 %all-to-all-start = ((bf16[8,144,128]{2,1,0:T(8,128)(2,1)}), bf16[8,144,128]{2,1,0:T(8,128)(2,1)S(1)}, u32[]{:S(2)}, u32[]{:S(2)}) async-start(bf16[8,144,128]{2,1,0:T(8,128)(2,1)} %get-tuple-element.15), calls=%async_computation | async-start | bytes 589824 | tf_op jit(solution)/shard_map/all_to_all | solution.py:245
  39.2 19.0 %collective-permute-start.4 = (bf16[8,128,128]{2,1,0:T(8,128)(2,1)S(1)}, bf16[8,128,128]{2,1,0:T(8,128)(2,1)S(1)}, u32[]{:S(2)}, u32[]{:S(2)}) collective-permute-start(bf16[8,128,128]{2,1,0:T(8,128)(2,1)S(1)} %all_to_all.10.own_ref), channel_id=1, source_target_pairs={{8,0},{9,1},{10,2},{11,3},{12,4},{13,5},{14,6},{15,7},{16,12},{17,... | collective-permute-start | bytes 786440 | tf_op jit(solution)/shard_map/ppermute | solution.py:246
  56.3 1.9 %copy-start = (bf16[8,144,128]{2,1,0:T(8,128)(2,1)}, bf16[8,144,128]{2,1,0:T(8,128)(2,1)S(1)}, u32[]{:S(2)}) copy-start(bf16[8,144,128]{2,1,0:T(8,128)(2,1)S(1)} %all-to-all-done.own_ref.flag_ref) | copy-start | bytes 884740
  56.3 17.9 %collective-permute-start = (bf16[8,144,128]{2,1,0:T(8,128)(2,1)S(1)}, bf16[8,144,128]{2,1,0:T(8,128)(2,1)S(1)}, u32[]{:S(2)}, u32[]{:S(2)}) collective-permute-start(bf16[8,144,128]{2,1,0:T(8,128)(2,1)S(1)} %all-to-all-done.own_ref.flag_ref), channel_id=1, source_target_pairs={{8,0},{9,1},{10,2},{11,3},{12,4},{13,5},{14,6},{15,7},{16,12},{17,... | collective-permute-start | bytes 884744 | tf_op jit(solution)/shard_map/ppermute | solution.py:246
  58.3 0.7 copy-start.9
  62.6 23.3 %collective-permute-start.5 = (bf16[512,128]{1,0:T(8,128)(2,1)}, bf16[512,128]{1,0:T(8,128)(2,1)S(1)}, u32[]{:S(2)}, u32[]{:S(2)}) collective-permute-start(bf16[512,128]{1,0:T(8,128)(2,1)} %get-tuple-element.22), channel_id=1, source_target_pairs={{0,1},{1,0},{2,3},{3,2},{4,5},{5,4},{6,7},{7,6},{8,9},{9,8},{10,11... | collective-permute-start | bytes 393224 | tf_op jit(solution)/shard_map/ppermute | solution.py:254
  68.9 19.8 %collective-permute-start.6 = (bf16[512,128]{1,0:T(8,128)(2,1)}, bf16[512,128]{1,0:T(8,128)(2,1)S(1)}, u32[]{:S(2)}, u32[]{:S(2)}) collective-permute-start(bf16[512,128]{1,0:T(8,128)(2,1)} %get-tuple-element.23), channel_id=1, source_target_pairs={{0,2},{1,3},{2,0},{3,1},{4,6},{5,7},{6,4},{7,5},{8,10},{9,11},{10,... | collective-permute-start | bytes 393224 | tf_op jit(solution)/shard_map/ppermute | solution.py:254
  72.2 16.6 %collective-permute-start.7 = (bf16[512,128]{1,0:T(8,128)(2,1)}, bf16[512,128]{1,0:T(8,128)(2,1)S(1)}, u32[]{:S(2)}, u32[]{:S(2)}) collective-permute-start(bf16[512,128]{1,0:T(8,128)(2,1)} %get-tuple-element.24), channel_id=1, source_target_pairs={{0,3},{1,2},{2,1},{3,0},{4,7},{5,6},{6,5},{7,4},{8,11},{9,10},{10,... | collective-permute-start | bytes 393224 | tf_op jit(solution)/shard_map/ppermute | solution.py:254
  74.3 0.7 copy-start.8
  78.6 10.2 %collective-permute-start.1 = (bf16[512,128]{1,0:T(8,128)(2,1)}, bf16[512,128]{1,0:T(8,128)(2,1)S(1)}, u32[]{:S(2)}, u32[]{:S(2)}) collective-permute-start(bf16[512,128]{1,0:T(8,128)(2,1)} %get-tuple-element.17), channel_id=1, source_target_pairs={{0,1},{1,0},{2,3},{3,2},{4,5},{5,4},{6,7},{7,6},{8,9},{9,8},{10,11... | collective-permute-start | bytes 393224 | tf_op jit(solution)/shard_map/ppermute | solution.py:254
  83.4 11.9 %collective-permute-start.2 = (bf16[512,128]{1,0:T(8,128)(2,1)}, bf16[512,128]{1,0:T(8,128)(2,1)S(1)}, u32[]{:S(2)}, u32[]{:S(2)}) collective-permute-start(bf16[512,128]{1,0:T(8,128)(2,1)} %get-tuple-element.18), channel_id=1, source_target_pairs={{0,2},{1,3},{2,0},{3,1},{4,6},{5,7},{6,4},{7,5},{8,10},{9,11},{10,... | collective-permute-start | bytes 393224 | tf_op jit(solution)/shard_map/ppermute | solution.py:254
  85.8 13.3 %copy-start.2 = (bf16[512,128]{1,0:T(8,128)(2,1)}, bf16[512,128]{1,0:T(8,128)(2,1)S(1)}, u32[]{:S(2)}) copy-start(bf16[512,128]{1,0:T(8,128)(2,1)S(1)} %collective-permute-done.5.refs_5_) | copy-start | bytes 393220
  85.8 13.3 %collective-permute-start.3 = (bf16[512,128]{1,0:T(8,128)(2,1)}, bf16[512,128]{1,0:T(8,128)(2,1)S(1)}, u32[]{:S(2)}, u32[]{:S(2)}) collective-permute-start(bf16[512,128]{1,0:T(8,128)(2,1)} %get-tuple-element.19), channel_id=1, source_target_pairs={{0,3},{1,2},{2,1},{3,0},{4,7},{5,6},{6,5},{7,4},{8,11},{9,10},{10,... | collective-permute-start | bytes 393224 | tf_op jit(solution)/shard_map/ppermute | solution.py:254
  88.8 10.3 %copy-start.3 = (bf16[512,128]{1,0:T(8,128)(2,1)}, bf16[512,128]{1,0:T(8,128)(2,1)S(1)}, u32[]{:S(2)}) copy-start(bf16[512,128]{1,0:T(8,128)(2,1)S(1)} %collective-permute-done.6.refs_6_) | copy-start | bytes 393220
  88.8 10.3 %copy-start.4 = (bf16[512,128]{1,0:T(8,128)(2,1)}, bf16[512,128]{1,0:T(8,128)(2,1)S(1)}, u32[]{:S(2)}) copy-start(bf16[512,128]{1,0:T(8,128)(2,1)S(1)} %collective-permute-done.7.refs_7_) | copy-start | bytes 393220
  88.8 10.3 %copy-start.5 = (bf16[512,128]{1,0:T(8,128)(2,1)}, bf16[512,128]{1,0:T(8,128)(2,1)S(1)}, u32[]{:S(2)}) copy-start(bf16[512,128]{1,0:T(8,128)(2,1)S(1)} %collective-permute-done.1.refs_1_) | copy-start | bytes 393220
  95.4 3.8 %copy-start.6 = (bf16[512,128]{1,0:T(8,128)(2,1)}, bf16[512,128]{1,0:T(8,128)(2,1)S(1)}, u32[]{:S(2)}) copy-start(bf16[512,128]{1,0:T(8,128)(2,1)S(1)} %collective-permute-done.2.refs_2_) | copy-start | bytes 393220
  99.1 0.7 copy-start.7

commit v3 on v2

--- a/solution.py
+++ b/solution.py
@@ -22,6 +22,7 @@
 BF16 = jnp.bfloat16
 VMEM = pl.BlockSpec(memory_space=pltpu.VMEM)
 SMEM = pl.BlockSpec(memory_space=pltpu.SMEM)
+SMALL = pltpu.CompilerParams(vmem_limit_bytes=16 * 2**20)
 BIG = pltpu.CompilerParams(vmem_limit_bytes=60 * 2**20)
 
 
@@ -98,9 +99,9 @@
                         outs[batch][dest] = value
 
 
-def stack_kernel(total_segs, first, par_ref, own_ref, halo_ref, flag_ref, *refs):
-    outs, scratch = refs[:QUADS], refs[QUADS]
-    half, quad = par_ref[0], par_ref[1]
+def stack_kernel(total_segs, first, own_ref, halo_ref, flag_ref, *refs):
+    outs, scratch = refs[:-1], refs[-1]
+    half, quad = lax.axis_index("h"), lax.axis_index("q")
     srcs, _, width = own_ref.shape
     depth = GROUP * 8
 
@@ -155,17 +156,21 @@
     for which in range(2):
         pl.when(half == which)(functools.partial(fill, which))
     for slot in range(QUADS):
-        start = pl.multiple_of((3 - (quad ^ slot)) * 512, 512)
-        outs[slot][...] = scratch[pl.ds(start, 512), :].astype(BF16)
-
-
-def turn_kernel(par_ref, *refs):
+        if len(outs) == 1:
+            outs[0][slot] = scratch[(3 - slot) * 512 : (4 - slot) * 512, :].astype(BF16)
+        else:
+            start = pl.multiple_of((3 - (quad ^ slot)) * 512, 512)
+            outs[slot][...] = scratch[pl.ds(start, 512), :].astype(BF16)
+
+
+def turn_kernel(*refs):
     parts, out_ref, scratch = refs[:-2], refs[-2], refs[-1]
-    quad = par_ref[1]
+    quad = lax.axis_index("q")
     count = out_ref.shape[0]
-    for index, ref in enumerate(parts):
-        batch, slot = index // QUADS, index % QUADS
-        group = (quad ^ slot) * BATCHES + batch
+    sources = [(quad ^ slot, 0, ref) for slot, ref in enumerate(parts[:QUADS])]
+    sources += [(source, 1, parts[QUADS].at[source]) for source in range(QUADS)]
+    for source, batch, ref in sources:
+        group = source * BATCHES + batch
         for row in range(count):
             for part in range(2):
                 start = pl.multiple_of(part * 128 + GROUP * group, GROUP)
@@ -204,29 +209,36 @@
     )(use, alive[None, :], raw, basis_columns(nsamp))
 
 
-def stack_pairs(par, own, halo, flags, total_segs, first):
+def stack_pairs(own, halo, flags, total_segs, first):
+    if first == 0:
+        shapes = [jax.ShapeDtypeStruct((QUADS, 512, OFFS), BF16)]
+    else:
+        shapes = [jax.ShapeDtypeStruct((512, OFFS), BF16)] * QUADS
     return pl.pallas_call(
         functools.partial(stack_kernel, total_segs, first),
-        out_shape=[jax.ShapeDtypeStruct((512, OFFS), BF16)] * QUADS,
-        in_specs=[SMEM] + [VMEM] * 3,
-        out_specs=[VMEM] * QUADS,
+        out_shape=shapes,
+        in_specs=[VMEM] * 3,
+        out_specs=[VMEM] * len(shapes),
         scratch_shapes=[pltpu.VMEM((512 * QUADS, OFFS), F32)],
-        cost_estimate=pl.CostEstimate(flops=2 * 8 * 256 * 256 * 256, bytes_accessed=2**20, transcendentals=0),
+        cost_estimate=pl.CostEstimate(flops=2 * 8 * 256 * 256 * 256 * 100, bytes_accessed=100 * 2**20, transcendentals=0),
+        compiler_params=SMALL,
         name="stack",
-    )(par, own, halo, flags)
-
-
-def turn_pieces(par, pieces, sub):
+    )(own, halo, flags)
+
+
+def turn_pieces(pieces, sub):
     steps = 2
     return pl.pallas_call(
         turn_kernel,
         out_shape=jax.ShapeDtypeStruct((sub, OFFS, 2 * BINS), BF16),
         grid=(steps,),
-        in_specs=[SMEM] + [pl.BlockSpec((512 // steps, OFFS), lambda step: (steps - 1 - step, 0))] * len(pieces),
+        in_specs=[pl.BlockSpec((512 // steps, OFFS), lambda step: (steps - 1 - step, 0))] * QUADS
+        + [pl.BlockSpec((QUADS, 512 // steps, OFFS), lambda step: (0, steps - 1 - step, 0))],
         out_specs=pl.BlockSpec((sub // steps, OFFS, 2 * BINS), lambda step: (step, 0, 0)),
         scratch_shapes=[pltpu.VMEM((sub // steps, 2 * BINS, OFFS), BF16)],
+        compiler_params=SMALL,
         name="turn",
-    )(par, *pieces)
+    )(*pieces)
 
 
 def shards(raw, alive, use):
@@ -234,7 +246,6 @@
     chans = lax.axis_size("chan")
     total_segs = seg_local * lax.axis_size("h") * lax.axis_size("q")
     axes = ("chan", "h", "q")
-    par = jnp.stack([lax.axis_index("h"), lax.axis_index("q")]).astype(jnp.int32)
 
     def index(chan, half, quad):
         return (chan * 2 + half) * QUADS + quad
@@ -247,13 +258,16 @@
     pieces = []
     for batch, (own, halo) in enumerate(zip(owns, halos)):
         first = FLAG_ROWS if batch == 0 else 0
-        stacked = stack_pairs(par, own, halo, owns[0], total_segs, first)
+        stacked = stack_pairs(own, halo, owns[0], total_segs, first)
+        if batch == 1:
+            pieces.append(lax.all_to_all(stacked[0], "q", 0, 0, tiled=True))
+            continue
         part = [stacked[0]] + [None] * (QUADS - 1)
         for slot in (2, 3, 1):
             pairs = [(index(c, h, q), index(c, h, q ^ slot)) for c, h, q in places]
             part[slot] = lax.ppermute(stacked[slot], axes, pairs)
         pieces += part
-    return turn_pieces(par, pieces, channels // (2 * QUADS))
+    return turn_pieces(pieces, channels // (2 * QUADS))
 
 
 def solution(mesh):

time: 103 us -> 98.7 us (0.958)
  the two profiles are of different devices: /device:TPU:32 before, /device:TPU:81 now
where the time goes in v3:
time: 98.7 us; the launch traced here: 98.3 us
  starting transfers between devices  32 us (32%)
  waiting for transfers between devices  30.6 us (31%)
  blocking collectives  25 us (25%)
  Pallas kernels  10.6 us (11%)
    all_to_all x1, blocking collectives, shards(): lax.all_to_all(message, ('h', 'q'), 0, 0, tiled=True)  25 us
    all_to_all x1, waiting for transfers between devices, shards(): lax.all_to_all(message, ('h', 'q'), 0, 0, tiled=True)  15.4 us
    ppermute x3, waiting for transfers between devices, shards(): part[slot] = lax.ppermute(stacked[slot], axes, pairs)  12.7 us
    ppermute x3, starting transfers between devices, shards(): part[slot] = lax.ppermute(stacked[slot], axes, pairs)  11.3 us
    ppermute x2, starting transfers between devices, shards(): halos = [lax.ppermute(own, axes, behind) for own in owns]  8.1 us
    all_to_all x1, starting transfers between devices, shards(): lax.all_to_all(message, ('h', 'q'), 0, 0, tiled=True)  7.95 us
    pallas_call x1, Pallas kernels, spectra(): pl.pallas_call(functools.partial(spectrum_kernel, nsamp), out_shape=[jax....  4.83 us
    all_to_all x1, starting transfers between devices, shards(): pieces.append(lax.all_to_all(stacked[0], 'q', 0, 0, tiled=True))  4.73 us
  transfers between devices with their start and end apart: 7, of which 4 were waited for; matrix products, arithmetic and copies ran while one was open for 0% of the time, Pallas kernels for 4%

profile of v3, /device:TPU:81, one launch (start us, length us, event | category | flops | bytes accessed | tf_op | source)
XLA Modules:
  0.0 98.3 jit_solution(9720706756531138809)
XLA Ops:
  0.0 4.8 %spectra.1 = (bf16[8,144,128]{2,1,0:T(8,128)(2,1)}, bf16[8,128,128]{2,1,0:T(8,128)(2,1)}) custom-call(s32[4]{0:T(128)} %use_ref.1, s32[1,128]{1,0:T(1,128)} %bitcast.1, bf16[128,4,3072]{2,1,0:T(4,128)(2,1)} %raw_ref.1, bf16[3072,256]{1,0:T(8,128)(2,1)} %constant.2.clone.basis_ref), custom_call_target="tpu_custom_call" | custom-call | tf_op jit(solution)/shard_map/spectra/pallas_call | solution.py:188
  4.8 25.0 %all_to_all.15.own_ref = bf16[8,128,128]{2,1,0:T(8,128)(2,1)S(1)} all-to-all(bf16[8,128,128]{2,1,0:T(8,128)(2,1)} %get-tuple-element.16), channel_id=1, replica_groups=mesh['chan'=64,'h'=2,'q'=4] {'h','q'}, dimensions={0} | all-to-all | bytes 524288 | tf_op jit(solution)/shard_map/all_to_all | solution.py:256
  29.8 7.9 %all-to-all-start = ((bf16[8,144,128]{2,1,0:T(8,128)(2,1)}), bf16[8,144,128]{2,1,0:T(8,128)(2,1)S(1)}, u32[]{:S(2)}, u32[]{:S(2)}) async-start(bf16[8,144,128]{2,1,0:T(8,128)(2,1)} %get-tuple-element.11), calls=%async_computation | async-start | bytes 589824 | tf_op jit(solution)/shard_map/all_to_all | solution.py:256
  37.8 3.6 %collective-permute-start.4 = (bf16[8,128,128]{2,1,0:T(8,128)(2,1)S(1)}, bf16[8,128,128]{2,1,0:T(8,128)(2,1)S(1)}, u32[]{:S(2)}, u32[]{:S(2)}) collective-permute-start(bf16[8,128,128]{2,1,0:T(8,128)(2,1)S(1)} %all_to_all.15.own_ref), channel_id=1, source_target_pairs={{8,0},{9,1},{10,2},{11,3},{12,4},{13,5},{14,6},{15,7},{16,12},{17,... | collective-permute-start | bytes 786440 | tf_op jit(solution)/shard_map/ppermute | solution.py:257
  41.3 15.4 %all-to-all-done.own_ref.flag_ref = bf16[8,144,128]{2,1,0:T(8,128)(2,1)S(1)} async-done(((bf16[8,144,128]{2,1,0:T(8,128)(2,1)}), bf16[8,144,128]{2,1,0:T(8,128)(2,1)S(1)}, u32[]{:S(2)}, u32[]{:S(2)}) %all-to-all-start) | async-done | bytes 294944 | tf_op jit(solution)/shard_map/all_to_all | solution.py:256
  56.8 4.5 %collective-permute-start = (bf16[8,144,128]{2,1,0:T(8,128)(2,1)S(1)}, bf16[8,144,128]{2,1,0:T(8,128)(2,1)S(1)}, u32[]{:S(2)}, u32[]{:S(2)}) collective-permute-start(bf16[8,144,128]{2,1,0:T(8,128)(2,1)S(1)} %all-to-all-done.own_ref.flag_ref), channel_id=1, source_target_pairs={{8,0},{9,1},{10,2},{11,3},{12,4},{13,5},{14,6},{15,7},{16,12},{17,... | collective-permute-start | bytes 884744 | tf_op jit(solution)/shard_map/ppermute | solution.py:257
  61.3 0.0 collective-permute-done.4.halo_ref
  61.3 2.5 %stack.3 = bf16[4,512,128]{2,1,0:T(8,128)(2,1)} custom-call(bf16[8,128,128]{2,1,0:T(8,128)(2,1)S(1)} %all_to_all.15.own_ref, bf16[8,128,128]{2,1,0:T(8,128)(2,1)S(1)} %collective-permute-done.4.halo_ref, bf16[8,144,128]{2,1,0:T(8,128)(2,1)S(1)} %all-to-all-done.own_ref.flag_ref), custom_call_target="tpu_custom_call" | custom-call | flops 26843545600 | bytes 104857600 | tf_op jit(solution)/shard_map/stack/pallas_call | solution.py:217
  63.8 4.7 %all-to-all-start.2 = ((bf16[4,512,128]{2,1,0:T(8,128)(2,1)}), bf16[4,512,128]{2,1,0:T(8,128)(2,1)S(1)}, u32[]{:S(2)}, u32[]{:S(2)}) async-start(bf16[4,512,128]{2,1,0:T(8,128)(2,1)} %stack.3), calls=%async_computation.2 | async-start | bytes 1048576 | tf_op jit(solution)/shard_map/all_to_all | solution.py:263
  68.5 2.5 %collective-permute-done.halo_ref = bf16[8,144,128]{2,1,0:T(8,128)(2,1)S(1)} collective-permute-done((bf16[8,144,128]{2,1,0:T(8,128)(2,1)S(1)}, bf16[8,144,128]{2,1,0:T(8,128)(2,1)S(1)}, u32[]{:S(2)}, u32[]{:S(2)}) %collective-permute-start) | collective-permute-done | bytes 294944 | tf_op jit(solution)/shard_map/ppermute | solution.py:257
  71.0 1.7 %stack.2 = (bf16[512,128]{1,0:T(8,128)(2,1)S(1)}, bf16[512,128]{1,0:T(8,128)(2,1)S(1)}, bf16[512,128]{1,0:T(8,128)(2,1)S(1)}, bf16[512,128]{1,0:T(8,128)(2,1)S(1)}) custom-call(bf16[8,144,128]{2,1,0:T(8,128)(2,1)S(1)} %all-to-all-done.own_ref.flag_ref, bf16[8,144,128]{2,1,0:T(8,128)(2,1)S(1)} %collective-permute-done.halo_ref, ...), custom_call_target="tpu_custom_call" | custom-call | flops 26843545600 | bytes 104857600 | tf_op jit(solution)/shard_map/stack/pallas_call | solution.py:217
  72.7 6.3 %collective-permute-start.1 = (bf16[512,128]{1,0:T(8,128)(2,1)S(1)}, bf16[512,128]{1,0:T(8,128)(2,1)S(1)}, u32[]{:S(2)}, u32[]{:S(2)}) collective-permute-start(bf16[512,128]{1,0:T(8,128)(2,1)S(1)} %get-tuple-element.13), channel_id=1, source_target_pairs={{0,1},{1,0},{2,3},{3,2},{4,5},{5,4},{6,7},{7,6},{8,9},{9,8},{10,11... | collective-permute-start | bytes 393224 | tf_op jit(solution)/shard_map/ppermute | solution.py:268
  79.0 1.9 %collective-permute-start.2 = (bf16[512,128]{1,0:T(8,128)(2,1)S(1)}, bf16[512,128]{1,0:T(8,128)(2,1)S(1)}, u32[]{:S(2)}, u32[]{:S(2)}) collective-permute-start(bf16[512,128]{1,0:T(8,128)(2,1)S(1)} %get-tuple-element.14), channel_id=1, source_target_pairs={{0,2},{1,3},{2,0},{3,1},{4,6},{5,7},{6,4},{7,5},{8,10},{9,11},{10,... | collective-permute-start | bytes 393224 | tf_op jit(solution)/shard_map/ppermute | solution.py:268
  80.9 3.1 %collective-permute-start.3 = (bf16[512,128]{1,0:T(8,128)(2,1)S(1)}, bf16[512,128]{1,0:T(8,128)(2,1)S(1)}, u32[]{:S(2)}, u32[]{:S(2)}) collective-permute-start(bf16[512,128]{1,0:T(8,128)(2,1)S(1)} %get-tuple-element.15), channel_id=1, source_target_pairs={{0,3},{1,2},{2,1},{3,0},{4,7},{5,6},{6,5},{7,4},{8,11},{9,10},{10,... | collective-permute-start | bytes 393224 | tf_op jit(solution)/shard_map/ppermute | solution.py:268
  84.0 0.0 collective-permute-done.1.refs_1_
  84.0 1.8 %collective-permute-done.2.refs_2_ = bf16[512,128]{1,0:T(8,128)(2,1)S(1)} collective-permute-done((bf16[512,128]{1,0:T(8,128)(2,1)S(1)}, bf16[512,128]{1,0:T(8,128)(2,1)S(1)}, u32[]{:S(2)}, u32[]{:S(2)}) %collective-permute-start.2) | collective-permute-done | bytes 131104 | tf_op jit(solution)/shard_map/ppermute | solution.py:268
  85.8 10.9 %collective-permute-done.3.refs_3_ = bf16[512,128]{1,0:T(8,128)(2,1)S(1)} collective-permute-done((bf16[512,128]{1,0:T(8,128)(2,1)S(1)}, bf16[512,128]{1,0:T(8,128)(2,1)S(1)}, u32[]{:S(2)}, u32[]{:S(2)}) %collective-permute-start.3) | collective-permute-done | bytes 131104 | tf_op jit(solution)/shard_map/ppermute | solution.py:268
  96.7 0.0 all-to-all-done.2.refs_4_
  96.7 1.6 %turn.1 = bf16[16,128,256]{2,1,0:T(8,128)(2,1)} custom-call(bf16[512,128]{1,0:T(8,128)(2,1)S(1)} %get-tuple-element.12.refs_0_, bf16[512,128]{1,0:T(8,128)(2,1)S(1)} %collective-permute-done.1.refs_1_, bf16[512,128]{1,0:T(8,128)(2,1)S(1)} %collective-permute-done.2.refs_2_, bf16[512,128]{1,0:T(8,128)(2,1)S(1)} %collective-permute-done.3.refs_3_, ...), custom_call_target="tpu_custom_call" | custom-call | tf_op jit(solution)/shard_map/turn/pallas_call | solution.py:231
Async XLA Ops:
  29.8 26.9 %all-to-all-start = ((bf16[8,144,128]{2,1,0:T(8,128)(2,1)}), bf16[8,144,128]{2,1,0:T(8,128)(2,1)S(1)}, u32[]{:S(2)}, u32[]{:S(2)}) async-start(bf16[8,144,128]{2,1,0:T(8,128)(2,1)} %get-tuple-element.11), calls=%async_computation | async-start | bytes 589824 | tf_op jit(solution)/shard_map/all_to_all | solution.py:256
  37.8 23.5 %collective-permute-start.4 = (bf16[8,128,128]{2,1,0:T(8,128)(2,1)S(1)}, bf16[8,128,128]{2,1,0:T(8,128)(2,1)S(1)}, u32[]{:S(2)}, u32[]{:S(2)}) collective-permute-start(bf16[8,128,128]{2,1,0:T(8,128)(2,1)S(1)} %all_to_all.15.own_ref), channel_id=1, source_target_pairs={{8,0},{9,1},{10,2},{11,3},{12,4},{13,5},{14,6},{15,7},{16,12},{17,... | collective-permute-start | bytes 786440 | tf_op jit(solution)/shard_map/ppermute | solution.py:257
  56.8 14.3 %collective-permute-start = (bf16[8,144,128]{2,1,0:T(8,128)(2,1)S(1)}, bf16[8,144,128]{2,1,0:T(8,128)(2,1)S(1)}, u32[]{:S(2)}, u32[]{:S(2)}) collective-permute-start(bf16[8,144,128]{2,1,0:T(8,128)(2,1)S(1)} %all-to-all-done.own_ref.flag_ref), channel_id=1, source_target_pairs={{8,0},{9,1},{10,2},{11,3},{12,4},{13,5},{14,6},{15,7},{16,12},{17,... | collective-permute-start | bytes 884744 | tf_op jit(solution)/shard_map/ppermute | solution.py:257
  63.8 32.9 %all-to-all-start.2 = ((bf16[4,512,128]{2,1,0:T(8,128)(2,1)}), bf16[4,512,128]{2,1,0:T(8,128)(2,1)S(1)}, u32[]{:S(2)}, u32[]{:S(2)}) async-start(bf16[4,512,128]{2,1,0:T(8,128)(2,1)} %stack.3), calls=%async_computation.2 | async-start | bytes 1048576 | tf_op jit(solution)/shard_map/all_to_all | solution.py:263
  72.7 11.3 %collective-permute-start.1 = (bf16[512,128]{1,0:T(8,128)(2,1)S(1)}, bf16[512,128]{1,0:T(8,128)(2,1)S(1)}, u32[]{:S(2)}, u32[]{:S(2)}) collective-permute-start(bf16[512,128]{1,0:T(8,128)(2,1)S(1)} %get-tuple-element.13), channel_id=1, source_target_pairs={{0,1},{1,0},{2,3},{3,2},{4,5},{5,4},{6,7},{7,6},{8,9},{9,8},{10,11... | collective-permute-start | bytes 393224 | tf_op jit(solution)/shard_map/ppermute | solution.py:268
  79.0 6.8 %collective-permute-start.2 = (bf16[512,128]{1,0:T(8,128)(2,1)S(1)}, bf16[512,128]{1,0:T(8,128)(2,1)S(1)}, u32[]{:S(2)}, u32[]{:S(2)}) collective-permute-start(bf16[512,128]{1,0:T(8,128)(2,1)S(1)} %get-tuple-element.14), channel_id=1, source_target_pairs={{0,2},{1,3},{2,0},{3,1},{4,6},{5,7},{6,4},{7,5},{8,10},{9,11},{10,... | collective-permute-start | bytes 393224 | tf_op jit(solution)/shard_map/ppermute | solution.py:268
  80.9 15.8 %collective-permute-start.3 = (bf16[512,128]{1,0:T(8,128)(2,1)S(1)}, bf16[512,128]{1,0:T(8,128)(2,1)S(1)}, u32[]{:S(2)}, u32[]{:S(2)}) collective-permute-start(bf16[512,128]{1,0:T(8,128)(2,1)S(1)} %get-tuple-element.15), channel_id=1, source_target_pairs={{0,3},{1,2},{2,1},{3,0},{4,7},{5,6},{6,5},{7,4},{8,11},{9,10},{10,... | collective-permute-start | bytes 393224 | tf_op jit(solution)/shard_map/ppermute | solution.py:268

commit v4 on v3

--- a/solution.py
+++ b/solution.py
@@ -105,13 +105,13 @@
     srcs, _, width = own_ref.shape
     depth = GROUP * 8
 
-    def inverse(ref):
-        value = ref[:, first : first + depth, :].astype(F32)
+    def inverse(value):
+        value = value.astype(F32)
         total = jnp.sum(value * value, axis=(0, 1))[None, :]
         return lax.rsqrt(total * (1.0 / (GROUP * total_segs)) + 1e-06)
 
-    own_scale = inverse(own_ref)
-    col_scale = jnp.concatenate([own_scale, inverse(halo_ref)], axis=1) * (1.0 / total_segs)
+    own_scale = inverse(own_ref[:, first : first + depth, :])
+    col_scale = jnp.concatenate([own_scale, inverse(halo_ref[...])], axis=1) * (1.0 / total_segs)
     pick = lax.broadcasted_iota(jnp.int32, (64, width), 1) == (
         64 * half + 63 - lax.broadcasted_iota(jnp.int32, (64, width), 0)
     )
@@ -141,7 +141,7 @@
     def fill(which):
         for pair in range(GROUP // 2):
             rows = slice(first + 16 * pair, first + 16 * pair + 16)
-            behind = halo_ref[:, rows, :].reshape(depth, width)
+            behind = halo_ref[:, 16 * pair : 16 * pair + 16, :].reshape(depth, width)
             left = lefts[64 * pair : 64 * pair + 64]
             left = jnp.concatenate([left[:, 128 * k : 128 * k + 128] for k in range(4)], axis=0)
             right = jnp.concatenate([owns[pair], behind], axis=1)
@@ -254,7 +254,7 @@
     behind = [(index(c, h, q), index(c - 1, h if c % 2 else 1 - h, q)) for c, h, q in places if c > 0]
 
     owns = [lax.all_to_all(message, ("h", "q"), 0, 0, tiled=True) for message in spectra(raw, alive, use)]
-    halos = [lax.ppermute(own, axes, behind) for own in owns]
+    halos = [lax.ppermute(own[:, -GROUP * 8 :], axes, behind) for own in owns]
     pieces = []
     for batch, (own, halo) in enumerate(zip(owns, halos)):
         first = FLAG_ROWS if batch == 0 else 0

time: 98.7 us -> 97.4 us (0.987)
  waiting for transfers between devices: 30.6 us -> 29.5 us
    ppermute x2, waiting for transfers between devices: 2.51 us -> 1.33 us  [shards(): halos = [lax.ppermute(own[:, -GROUP * 8:], axes, behind) for own in owns]]
where the time goes in v4:
time: 97.4 us; the launch traced here: 96.9 us
  starting transfers between devices  31.8 us (33%)
  waiting for transfers between devices  29.5 us (30%)
  blocking collectives  25 us (26%)
  Pallas kernels  10.6 us (11%)
    all_to_all x1, blocking collectives, shards(): lax.all_to_all(message, ('h', 'q'), 0, 0, tiled=True)  25 us
    all_to_all x1, waiting for transfers between devices, shards(): lax.all_to_all(message, ('h', 'q'), 0, 0, tiled=True)  15.4 us
    ppermute x3, waiting for transfers between devices, shards(): part[slot] = lax.ppermute(stacked[slot], axes, pairs)  12.7 us
    ppermute x3, starting transfers between devices, shards(): part[slot] = lax.ppermute(stacked[slot], axes, pairs)  11 us
    ppermute x2, starting transfers between devices, shards(): halos = [lax.ppermute(own[:, -GROUP * 8:], axes, behind) for own in owns]  8.11 us
    all_to_all x1, starting transfers between devices, shards(): lax.all_to_all(message, ('h', 'q'), 0, 0, tiled=True)  7.95 us
    pallas_call x1, Pallas kernels, spectra(): pl.pallas_call(functools.partial(spectrum_kernel, nsamp), out_shape=[jax....  4.83 us
    all_to_all x1, starting transfers between devices, shards(): pieces.append(lax.all_to_all(stacked[0], 'q', 0, 0, tiled=True))  4.74 us
  transfers between devices with their start and end apart: 7, of which 4 were waited for; matrix products, arithmetic and copies ran while one was open for 0% of the time, Pallas kernels for 4%

profile of v4, /device:TPU:81, one launch (start us, length us, event | category | flops | bytes accessed | tf_op | source)
XLA Modules:
  0.0 96.9 jit_solution(5542113863744767147)
XLA Ops:
  0.0 4.8 %spectra.1 = (bf16[8,144,128]{2,1,0:T(8,128)(2,1)}, bf16[8,128,128]{2,1,0:T(8,128)(2,1)}) custom-call(s32[4]{0:T(128)} %use_ref.1, s32[1,128]{1,0:T(1,128)} %bitcast.1, bf16[128,4,3072]{2,1,0:T(4,128)(2,1)} %raw_ref.1, bf16[3072,256]{1,0:T(8,128)(2,1)} %constant.2.clone.basis_ref), custom_call_target="tpu_custom_call" | custom-call | tf_op jit(solution)/shard_map/spectra/pallas_call | solution.py:188
  4.8 25.0 %all_to_all.15.own_ref = bf16[8,128,128]{2,1,0:T(8,128)(2,1)S(1)} all-to-all(bf16[8,128,128]{2,1,0:T(8,128)(2,1)} %get-tuple-element.16), channel_id=1, replica_groups=mesh['chan'=64,'h'=2,'q'=4] {'h','q'}, dimensions={0} | all-to-all | bytes 524288 | tf_op jit(solution)/shard_map/all_to_all | solution.py:256
  29.8 7.9 %all-to-all-start = ((bf16[8,144,128]{2,1,0:T(8,128)(2,1)}), bf16[8,144,128]{2,1,0:T(8,128)(2,1)S(1)}, u32[]{:S(2)}, u32[]{:S(2)}) async-start(bf16[8,144,128]{2,1,0:T(8,128)(2,1)} %get-tuple-element.11), calls=%async_computation | async-start | bytes 589824 | tf_op jit(solution)/shard_map/all_to_all | solution.py:256
  37.8 3.6 %collective-permute-start.4 = (bf16[8,128,128]{2,1,0:T(8,128)(2,1)S(1)}, bf16[8,128,128]{2,1,0:T(8,128)(2,1)S(1)}, u32[]{:S(2)}, u32[]{:S(2)}) collective-permute-start(bf16[8,128,128]{2,1,0:T(8,128)(2,1)S(1)} %all_to_all.15.own_ref), channel_id=1, source_target_pairs={{8,0},{9,1},{10,2},{11,3},{12,4},{13,5},{14,6},{15,7},{16,12},{17,... | collective-permute-start | bytes 786440 | tf_op jit(solution)/shard_map/ppermute | solution.py:257
  41.3 15.4 %all-to-all-done.own_ref.flag_ref = bf16[8,144,128]{2,1,0:T(8,128)(2,1)S(1)} async-done(((bf16[8,144,128]{2,1,0:T(8,128)(2,1)}), bf16[8,144,128]{2,1,0:T(8,128)(2,1)S(1)}, u32[]{:S(2)}, u32[]{:S(2)}) %all-to-all-start) | async-done | bytes 294944 | tf_op jit(solution)/shard_map/all_to_all | solution.py:256
  56.8 4.6 %collective-permute-start = (bf16[8,128,128]{2,1,0:T(8,128)(2,1)S(1)}, bf16[8,128,128]{2,1,0:T(8,128)(2,1)S(1)}, u32[]{:S(2)}, u32[]{:S(2)}) collective-permute-start(bf16[8,128,128]{2,1,0:T(8,128)(2,1)S(1)} %slice.4), channel_id=1, source_target_pairs={{8,0},{9,1},{10,2},{11,3},{12,4},{13,5},{14,6},{15,7},{16,12},{17,... | collective-permute-start | bytes 786440 | tf_op jit(solution)/shard_map/ppermute | solution.py:257
  61.3 0.0 collective-permute-done.4.halo_ref
  61.4 2.5 %stack.3 = bf16[4,512,128]{2,1,0:T(8,128)(2,1)} custom-call(bf16[8,128,128]{2,1,0:T(8,128)(2,1)S(1)} %all_to_all.15.own_ref, bf16[8,128,128]{2,1,0:T(8,128)(2,1)S(1)} %collective-permute-done.4.halo_ref, bf16[8,144,128]{2,1,0:T(8,128)(2,1)S(1)} %all-to-all-done.own_ref.flag_ref), custom_call_target="tpu_custom_call" | custom-call | flops 26843545600 | bytes 104857600 | tf_op jit(solution)/shard_map/stack/pallas_call | solution.py:217
  63.8 4.7 %all-to-all-start.2 = ((bf16[4,512,128]{2,1,0:T(8,128)(2,1)}), bf16[4,512,128]{2,1,0:T(8,128)(2,1)S(1)}, u32[]{:S(2)}, u32[]{:S(2)}) async-start(bf16[4,512,128]{2,1,0:T(8,128)(2,1)} %stack.3), calls=%async_computation.2 | async-start | bytes 1048576 | tf_op jit(solution)/shard_map/all_to_all | solution.py:263
  68.6 1.3 %collective-permute-done.halo_ref = bf16[8,128,128]{2,1,0:T(8,128)(2,1)S(1)} collective-permute-done((bf16[8,128,128]{2,1,0:T(8,128)(2,1)S(1)}, bf16[8,128,128]{2,1,0:T(8,128)(2,1)S(1)}, u32[]{:S(2)}, u32[]{:S(2)}) %collective-permute-start) | collective-permute-done | bytes 262176 | tf_op jit(solution)/shard_map/ppermute | solution.py:257
  69.9 1.7 %stack.2 = (bf16[512,128]{1,0:T(8,128)(2,1)S(1)}, bf16[512,128]{1,0:T(8,128)(2,1)S(1)}, bf16[512,128]{1,0:T(8,128)(2,1)S(1)}, bf16[512,128]{1,0:T(8,128)(2,1)S(1)}) custom-call(bf16[8,144,128]{2,1,0:T(8,128)(2,1)S(1)} %all-to-all-done.own_ref.flag_ref, bf16[8,128,128]{2,1,0:T(8,128)(2,1)S(1)} %collective-permute-done.halo_ref, ...), custom_call_target="tpu_custom_call" | custom-call | flops 26843545600 | bytes 104857600 | tf_op jit(solution)/shard_map/stack/pallas_call | solution.py:217
  71.6 6.0 %collective-permute-start.1 = (bf16[512,128]{1,0:T(8,128)(2,1)S(1)}, bf16[512,128]{1,0:T(8,128)(2,1)S(1)}, u32[]{:S(2)}, u32[]{:S(2)}) collective-permute-start(bf16[512,128]{1,0:T(8,128)(2,1)S(1)} %get-tuple-element.13), channel_id=1, source_target_pairs={{0,1},{1,0},{2,3},{3,2},{4,5},{5,4},{6,7},{7,6},{8,9},{9,8},{10,11... | collective-permute-start | bytes 393224 | tf_op jit(solution)/shard_map/ppermute | solution.py:268
  77.6 1.9 %collective-permute-start.2 = (bf16[512,128]{1,0:T(8,128)(2,1)S(1)}, bf16[512,128]{1,0:T(8,128)(2,1)S(1)}, u32[]{:S(2)}, u32[]{:S(2)}) collective-permute-start(bf16[512,128]{1,0:T(8,128)(2,1)S(1)} %get-tuple-element.14), channel_id=1, source_target_pairs={{0,2},{1,3},{2,0},{3,1},{4,6},{5,7},{6,4},{7,5},{8,10},{9,11},{10,... | collective-permute-start | bytes 393224 | tf_op jit(solution)/shard_map/ppermute | solution.py:268
  79.5 3.1 %collective-permute-start.3 = (bf16[512,128]{1,0:T(8,128)(2,1)S(1)}, bf16[512,128]{1,0:T(8,128)(2,1)S(1)}, u32[]{:S(2)}, u32[]{:S(2)}) collective-permute-start(bf16[512,128]{1,0:T(8,128)(2,1)S(1)} %get-tuple-element.15), channel_id=1, source_target_pairs={{0,3},{1,2},{2,1},{3,0},{4,7},{5,6},{6,5},{7,4},{8,11},{9,10},{10,... | collective-permute-start | bytes 393224 | tf_op jit(solution)/shard_map/ppermute | solution.py:268
  82.6 0.0 collective-permute-done.1.refs_1_
  82.6 3.3 %collective-permute-done.2.refs_2_ = bf16[512,128]{1,0:T(8,128)(2,1)S(1)} collective-permute-done((bf16[512,128]{1,0:T(8,128)(2,1)S(1)}, bf16[512,128]{1,0:T(8,128)(2,1)S(1)}, u32[]{:S(2)}, u32[]{:S(2)}) %collective-permute-start.2) | collective-permute-done | bytes 131104 | tf_op jit(solution)/shard_map/ppermute | solution.py:268
  85.9 9.4 %collective-permute-done.3.refs_3_ = bf16[512,128]{1,0:T(8,128)(2,1)S(1)} collective-permute-done((bf16[512,128]{1,0:T(8,128)(2,1)S(1)}, bf16[512,128]{1,0:T(8,128)(2,1)S(1)}, u32[]{:S(2)}, u32[]{:S(2)}) %collective-permute-start.3) | collective-permute-done | bytes 131104 | tf_op jit(solution)/shard_map/ppermute | solution.py:268
  95.3 0.0 all-to-all-done.2.refs_4_
  95.3 1.6 %turn.1 = bf16[16,128,256]{2,1,0:T(8,128)(2,1)} custom-call(bf16[512,128]{1,0:T(8,128)(2,1)S(1)} %get-tuple-element.12.refs_0_, bf16[512,128]{1,0:T(8,128)(2,1)S(1)} %collective-permute-done.1.refs_1_, bf16[512,128]{1,0:T(8,128)(2,1)S(1)} %collective-permute-done.2.refs_2_, bf16[512,128]{1,0:T(8,128)(2,1)S(1)} %collective-permute-done.3.refs_3_, ...), custom_call_target="tpu_custom_call" | custom-call | tf_op jit(solution)/shard_map/turn/pallas_call | solution.py:231
  (1 shorter events, 0.0 us)
Async XLA Ops:
  29.8 26.9 %all-to-all-start = ((bf16[8,144,128]{2,1,0:T(8,128)(2,1)}), bf16[8,144,128]{2,1,0:T(8,128)(2,1)S(1)}, u32[]{:S(2)}, u32[]{:S(2)}) async-start(bf16[8,144,128]{2,1,0:T(8,128)(2,1)} %get-tuple-element.11), calls=%async_computation | async-start | bytes 589824 | tf_op jit(solution)/shard_map/all_to_all | solution.py:256
  37.8 23.6 %collective-permute-start.4 = (bf16[8,128,128]{2,1,0:T(8,128)(2,1)S(1)}, bf16[8,128,128]{2,1,0:T(8,128)(2,1)S(1)}, u32[]{:S(2)}, u32[]{:S(2)}) collective-permute-start(bf16[8,128,128]{2,1,0:T(8,128)(2,1)S(1)} %all_to_all.15.own_ref), channel_id=1, source_target_pairs={{8,0},{9,1},{10,2},{11,3},{12,4},{13,5},{14,6},{15,7},{16,12},{17,... | collective-permute-start | bytes 786440 | tf_op jit(solution)/shard_map/ppermute | solution.py:257
  56.8 13.1 %collective-permute-start = (bf16[8,128,128]{2,1,0:T(8,128)(2,1)S(1)}, bf16[8,128,128]{2,1,0:T(8,128)(2,1)S(1)}, u32[]{:S(2)}, u32[]{:S(2)}) collective-permute-start(bf16[8,128,128]{2,1,0:T(8,128)(2,1)S(1)} %slice.4), channel_id=1, source_target_pairs={{8,0},{9,1},{10,2},{11,3},{12,4},{13,5},{14,6},{15,7},{16,12},{17,... | collective-permute-start | bytes 786440 | tf_op jit(solution)/shard_map/ppermute | solution.py:257
  63.8 31.5 %all-to-all-start.2 = ((bf16[4,512,128]{2,1,0:T(8,128)(2,1)}), bf16[4,512,128]{2,1,0:T(8,128)(2,1)S(1)}, u32[]{:S(2)}, u32[]{:S(2)}) async-start(bf16[4,512,128]{2,1,0:T(8,128)(2,1)} %stack.3), calls=%async_computation.2 | async-start | bytes 1048576 | tf_op jit(solution)/shard_map/all_to_all | solution.py:263
  71.6 11.0 %collective-permute-start.1 = (bf16[512,128]{1,0:T(8,128)(2,1)S(1)}, bf16[512,128]{1,0:T(8,128)(2,1)S(1)}, u32[]{:S(2)}, u32[]{:S(2)}) collective-permute-start(bf16[512,128]{1,0:T(8,128)(2,1)S(1)} %get-tuple-element.13), channel_id=1, source_target_pairs={{0,1},{1,0},{2,3},{3,2},{4,5},{5,4},{6,7},{7,6},{8,9},{9,8},{10,11... | collective-permute-start | bytes 393224 | tf_op jit(solution)/shard_map/ppermute | solution.py:268
  77.6 8.3 %collective-permute-start.2 = (bf16[512,128]{1,0:T(8,128)(2,1)S(1)}, bf16[512,128]{1,0:T(8,128)(2,1)S(1)}, u32[]{:S(2)}, u32[]{:S(2)}) collective-permute-start(bf16[512,128]{1,0:T(8,128)(2,1)S(1)} %get-tuple-element.14), channel_id=1, source_target_pairs={{0,2},{1,3},{2,0},{3,1},{4,6},{5,7},{6,4},{7,5},{8,10},{9,11},{10,... | collective-permute-start | bytes 393224 | tf_op jit(solution)/shard_map/ppermute | solution.py:268
  79.5 15.8 %collective-permute-start.3 = (bf16[512,128]{1,0:T(8,128)(2,1)S(1)}, bf16[512,128]{1,0:T(8,128)(2,1)S(1)}, u32[]{:S(2)}, u32[]{:S(2)}) collective-permute-start(bf16[512,128]{1,0:T(8,128)(2,1)S(1)} %get-tuple-element.15), channel_id=1, source_target_pairs={{0,3},{1,2},{2,1},{3,0},{4,7},{5,6},{6,5},{7,4},{8,11},{9,10},{10,... | collective-permute-start | bytes 393224 | tf_op jit(solution)/shard_map/ppermute | solution.py:268

commit v5 on v4

--- a/solution.py
+++ b/solution.py
@@ -59,13 +59,13 @@
     @pl.when(step == 0)
     def _():
         for col in range(2):
-            spec[col] = product[:, 128 * col : 128 * col + 128]
+            spec[col, : channels * segs] = product[:, 128 * col : 128 * col + 128]
         square[...] = squares
 
     @pl.when(step > 0)
     def _():
         for col in range(2):
-            spec[col] += product[:, 128 * col : 128 * col + 128]
+            spec[col, : channels * segs] += product[:, 128 * col : 128 * col + 128]
         square[...] += squares
 
     @pl.when(step == pl.num_programs(0) - 1)
@@ -73,7 +73,7 @@
         meansq = jnp.sum(square[...], axis=1, keepdims=True) * (1.0 / nsamp)
         scale = lax.rsqrt(meansq + 1e-06)
         for col in range(2):
-            spec[col] = jnp.where(scale > 0, spec[col] * scale, 0.0)
+            spec[col, : channels * segs] = jnp.where(scale > 0, spec[col, : channels * segs] * scale, 0.0)
         width = 2 * 128
         alive = alive_ref[...].astype(F32)
         for seg in range(segs):
@@ -200,9 +200,9 @@
         ],
         out_specs=[VMEM] * BATCHES,
         scratch_shapes=[
-            pltpu.VMEM((2, channels * segs, BINS), F32),
+            pltpu.VMEM((2, channels * segs + 8, BINS), F32),
             pltpu.VMEM((channels * segs, 128), F32),
-            pltpu.VMEM((2 * BINS * segs, channels), F32),
+            pltpu.VMEM((2 * BINS * segs + 8, channels), F32),
         ],
         compiler_params=BIG,
         name="spectra",
@@ -219,7 +219,7 @@
         out_shape=shapes,
         in_specs=[VMEM] * 3,
         out_specs=[VMEM] * len(shapes),
-        scratch_shapes=[pltpu.VMEM((512 * QUADS, OFFS), F32)],
+        scratch_shapes=[pltpu.VMEM((512 * QUADS + 32, OFFS), F32)],
         cost_estimate=pl.CostEstimate(flops=2 * 8 * 256 * 256 * 256 * 100, bytes_accessed=100 * 2**20, transcendentals=0),
         compiler_params=SMALL,
         name="stack",
@@ -263,7 +263,7 @@
             pieces.append(lax.all_to_all(stacked[0], "q", 0, 0, tiled=True))
             continue
         part = [stacked[0]] + [None] * (QUADS - 1)
-        for slot in (2, 3, 1):
+        for slot in (1, 3, 2):
             pairs = [(index(c, h, q), index(c, h, q ^ slot)) for c, h, q in places]
             part[slot] = lax.ppermute(stacked[slot], axes, pairs)
         pieces += part

time: 97.4 us -> 97.4 us (level)
  no operation moved by 1% of the time
where the time goes in v5:
time: 97.4 us; the launch traced here: 96.9 us
  starting transfers between devices  31.8 us (33%)
  waiting for transfers between devices  29.5 us (30%)
  blocking collectives  25 us (26%)
  Pallas kernels  10.5 us (11%)
    all_to_all x1, blocking collectives, shards(): lax.all_to_all(message, ('h', 'q'), 0, 0, tiled=True)  25 us
    all_to_all x1, waiting for transfers between devices, shards(): lax.all_to_all(message, ('h', 'q'), 0, 0, tiled=True)  15.4 us
    ppermute x3, waiting for transfers between devices, shards(): part[slot] = lax.ppermute(stacked[slot], axes, pairs)  12.7 us
    ppermute x3, starting transfers between devices, shards(): part[slot] = lax.ppermute(stacked[slot], axes, pairs)  11 us
    ppermute x2, starting transfers between devices, shards(): halos = [lax.ppermute(own[:, -GROUP * 8:], axes, behind) for own in owns]  8.11 us
    all_to_all x1, starting transfers between devices, shards(): lax.all_to_all(message, ('h', 'q'), 0, 0, tiled=True)  7.94 us
    pallas_call x1, Pallas kernels, spectra(): pl.pallas_call(functools.partial(spectrum_kernel, nsamp), out_shape=[jax....  4.82 us
    all_to_all x1, starting transfers between devices, shards(): pieces.append(lax.all_to_all(stacked[0], 'q', 0, 0, tiled=True))  4.74 us
  transfers between devices with their start and end apart: 7, of which 4 were waited for; matrix products, arithmetic and copies ran while one was open for 0% of the time, Pallas kernels for 4%

profile of v5, /device:TPU:81, one launch (start us, length us, event | category | flops | bytes accessed | tf_op | source)
XLA Modules:
  0.0 96.9 jit_solution(13702726838814850609)
XLA Ops:
  0.0 4.8 %spectra.1 = (bf16[8,144,128]{2,1,0:T(8,128)(2,1)}, bf16[8,128,128]{2,1,0:T(8,128)(2,1)}) custom-call(s32[4]{0:T(128)} %use_ref.1, s32[1,128]{1,0:T(1,128)} %bitcast.1, bf16[128,4,3072]{2,1,0:T(4,128)(2,1)} %raw_ref.1, bf16[3072,256]{1,0:T(8,128)(2,1)} %constant.2.clone.basis_ref), custom_call_target="tpu_custom_call" | custom-call | tf_op jit(solution)/shard_map/spectra/pallas_call | solution.py:188
  4.8 25.0 %all_to_all.15.own_ref = bf16[8,128,128]{2,1,0:T(8,128)(2,1)S(1)} all-to-all(bf16[8,128,128]{2,1,0:T(8,128)(2,1)} %get-tuple-element.16), channel_id=1, replica_groups=mesh['chan'=64,'h'=2,'q'=4] {'h','q'}, dimensions={0} | all-to-all | bytes 524288 | tf_op jit(solution)/shard_map/all_to_all | solution.py:256
  29.8 7.9 %all-to-all-start = ((bf16[8,144,128]{2,1,0:T(8,128)(2,1)}), bf16[8,144,128]{2,1,0:T(8,128)(2,1)S(1)}, u32[]{:S(2)}, u32[]{:S(2)}) async-start(bf16[8,144,128]{2,1,0:T(8,128)(2,1)} %get-tuple-element.11), calls=%async_computation | async-start | bytes 589824 | tf_op jit(solution)/shard_map/all_to_all | solution.py:256
  37.8 3.6 %collective-permute-start.4 = (bf16[8,128,128]{2,1,0:T(8,128)(2,1)S(1)}, bf16[8,128,128]{2,1,0:T(8,128)(2,1)S(1)}, u32[]{:S(2)}, u32[]{:S(2)}) collective-permute-start(bf16[8,128,128]{2,1,0:T(8,128)(2,1)S(1)} %all_to_all.15.own_ref), channel_id=1, source_target_pairs={{8,0},{9,1},{10,2},{11,3},{12,4},{13,5},{14,6},{15,7},{16,12},{17,... | collective-permute-start | bytes 786440 | tf_op jit(solution)/shard_map/ppermute | solution.py:257
  41.3 15.4 %all-to-all-done.own_ref.flag_ref = bf16[8,144,128]{2,1,0:T(8,128)(2,1)S(1)} async-done(((bf16[8,144,128]{2,1,0:T(8,128)(2,1)}), bf16[8,144,128]{2,1,0:T(8,128)(2,1)S(1)}, u32[]{:S(2)}, u32[]{:S(2)}) %all-to-all-start) | async-done | bytes 294944 | tf_op jit(solution)/shard_map/all_to_all | solution.py:256
  56.8 4.6 %collective-permute-start = (bf16[8,128,128]{2,1,0:T(8,128)(2,1)S(1)}, bf16[8,128,128]{2,1,0:T(8,128)(2,1)S(1)}, u32[]{:S(2)}, u32[]{:S(2)}) collective-permute-start(bf16[8,128,128]{2,1,0:T(8,128)(2,1)S(1)} %slice.4), channel_id=1, source_target_pairs={{8,0},{9,1},{10,2},{11,3},{12,4},{13,5},{14,6},{15,7},{16,12},{17,... | collective-permute-start | bytes 786440 | tf_op jit(solution)/shard_map/ppermute | solution.py:257
  61.3 0.0 collective-permute-done.4.halo_ref
  61.4 2.5 %stack.3 = bf16[4,512,128]{2,1,0:T(8,128)(2,1)} custom-call(bf16[8,128,128]{2,1,0:T(8,128)(2,1)S(1)} %all_to_all.15.own_ref, bf16[8,128,128]{2,1,0:T(8,128)(2,1)S(1)} %collective-permute-done.4.halo_ref, bf16[8,144,128]{2,1,0:T(8,128)(2,1)S(1)} %all-to-all-done.own_ref.flag_ref), custom_call_target="tpu_custom_call" | custom-call | flops 26843545600 | bytes 104857600 | tf_op jit(solution)/shard_map/stack/pallas_call | solution.py:217
  63.8 4.7 %all-to-all-start.2 = ((bf16[4,512,128]{2,1,0:T(8,128)(2,1)}), bf16[4,512,128]{2,1,0:T(8,128)(2,1)S(1)}, u32[]{:S(2)}, u32[]{:S(2)}) async-start(bf16[4,512,128]{2,1,0:T(8,128)(2,1)} %stack.3), calls=%async_computation.2 | async-start | bytes 1048576 | tf_op jit(solution)/shard_map/all_to_all | solution.py:263
  68.6 1.3 %collective-permute-done.halo_ref = bf16[8,128,128]{2,1,0:T(8,128)(2,1)S(1)} collective-permute-done((bf16[8,128,128]{2,1,0:T(8,128)(2,1)S(1)}, bf16[8,128,128]{2,1,0:T(8,128)(2,1)S(1)}, u32[]{:S(2)}, u32[]{:S(2)}) %collective-permute-start) | collective-permute-done | bytes 262176 | tf_op jit(solution)/shard_map/ppermute | solution.py:257
  69.9 1.7 %stack.2 = (bf16[512,128]{1,0:T(8,128)(2,1)S(1)}, bf16[512,128]{1,0:T(8,128)(2,1)S(1)}, bf16[512,128]{1,0:T(8,128)(2,1)S(1)}, bf16[512,128]{1,0:T(8,128)(2,1)S(1)}) custom-call(bf16[8,144,128]{2,1,0:T(8,128)(2,1)S(1)} %all-to-all-done.own_ref.flag_ref, bf16[8,128,128]{2,1,0:T(8,128)(2,1)S(1)} %collective-permute-done.halo_ref, ...), custom_call_target="tpu_custom_call" | custom-call | flops 26843545600 | bytes 104857600 | tf_op jit(solution)/shard_map/stack/pallas_call | solution.py:217
  71.6 6.0 %collective-permute-start.1 = (bf16[512,128]{1,0:T(8,128)(2,1)S(1)}, bf16[512,128]{1,0:T(8,128)(2,1)S(1)}, u32[]{:S(2)}, u32[]{:S(2)}) collective-permute-start(bf16[512,128]{1,0:T(8,128)(2,1)S(1)} %get-tuple-element.13), channel_id=1, source_target_pairs={{0,1},{1,0},{2,3},{3,2},{4,5},{5,4},{6,7},{7,6},{8,9},{9,8},{10,11... | collective-permute-start | bytes 393224 | tf_op jit(solution)/shard_map/ppermute | solution.py:268
  77.6 1.9 %collective-permute-start.2 = (bf16[512,128]{1,0:T(8,128)(2,1)S(1)}, bf16[512,128]{1,0:T(8,128)(2,1)S(1)}, u32[]{:S(2)}, u32[]{:S(2)}) collective-permute-start(bf16[512,128]{1,0:T(8,128)(2,1)S(1)} %get-tuple-element.14), channel_id=1, source_target_pairs={{0,2},{1,3},{2,0},{3,1},{4,6},{5,7},{6,4},{7,5},{8,10},{9,11},{10,... | collective-permute-start | bytes 393224 | tf_op jit(solution)/shard_map/ppermute | solution.py:268
  79.5 3.1 %collective-permute-start.3 = (bf16[512,128]{1,0:T(8,128)(2,1)S(1)}, bf16[512,128]{1,0:T(8,128)(2,1)S(1)}, u32[]{:S(2)}, u32[]{:S(2)}) collective-permute-start(bf16[512,128]{1,0:T(8,128)(2,1)S(1)} %get-tuple-element.15), channel_id=1, source_target_pairs={{0,3},{1,2},{2,1},{3,0},{4,7},{5,6},{6,5},{7,4},{8,11},{9,10},{10,... | collective-permute-start | bytes 393224 | tf_op jit(solution)/shard_map/ppermute | solution.py:268
  82.6 0.0 collective-permute-done.1.refs_1_
  82.6 3.3 %collective-permute-done.2.refs_2_ = bf16[512,128]{1,0:T(8,128)(2,1)S(1)} collective-permute-done((bf16[512,128]{1,0:T(8,128)(2,1)S(1)}, bf16[512,128]{1,0:T(8,128)(2,1)S(1)}, u32[]{:S(2)}, u32[]{:S(2)}) %collective-permute-start.2) | collective-permute-done | bytes 131104 | tf_op jit(solution)/shard_map/ppermute | solution.py:268
  85.9 9.4 %collective-permute-done.3.refs_3_ = bf16[512,128]{1,0:T(8,128)(2,1)S(1)} collective-permute-done((bf16[512,128]{1,0:T(8,128)(2,1)S(1)}, bf16[512,128]{1,0:T(8,128)(2,1)S(1)}, u32[]{:S(2)}, u32[]{:S(2)}) %collective-permute-start.3) | collective-permute-done | bytes 131104 | tf_op jit(solution)/shard_map/ppermute | solution.py:268
  95.3 0.0 all-to-all-done.2.refs_4_
  95.3 1.6 %turn.1 = bf16[16,128,256]{2,1,0:T(8,128)(2,1)} custom-call(bf16[512,128]{1,0:T(8,128)(2,1)S(1)} %get-tuple-element.12.refs_0_, bf16[512,128]{1,0:T(8,128)(2,1)S(1)} %collective-permute-done.1.refs_1_, bf16[512,128]{1,0:T(8,128)(2,1)S(1)} %collective-permute-done.2.refs_2_, bf16[512,128]{1,0:T(8,128)(2,1)S(1)} %collective-permute-done.3.refs_3_, ...), custom_call_target="tpu_custom_call" | custom-call | tf_op jit(solution)/shard_map/turn/pallas_call | solution.py:231
  (1 shorter events, 0.0 us)
Async XLA Ops:
  29.8 26.9 %all-to-all-start = ((bf16[8,144,128]{2,1,0:T(8,128)(2,1)}), bf16[8,144,128]{2,1,0:T(8,128)(2,1)S(1)}, u32[]{:S(2)}, u32[]{:S(2)}) async-start(bf16[8,144,128]{2,1,0:T(8,128)(2,1)} %get-tuple-element.11), calls=%async_computation | async-start | bytes 589824 | tf_op jit(solution)/shard_map/all_to_all | solution.py:256
  37.8 23.6 %collective-permute-start.4 = (bf16[8,128,128]{2,1,0:T(8,128)(2,1)S(1)}, bf16[8,128,128]{2,1,0:T(8,128)(2,1)S(1)}, u32[]{:S(2)}, u32[]{:S(2)}) collective-permute-start(bf16[8,128,128]{2,1,0:T(8,128)(2,1)S(1)} %all_to_all.15.own_ref), channel_id=1, source_target_pairs={{8,0},{9,1},{10,2},{11,3},{12,4},{13,5},{14,6},{15,7},{16,12},{17,... | collective-permute-start | bytes 786440 | tf_op jit(solution)/shard_map/ppermute | solution.py:257
  56.8 13.1 %collective-permute-start = (bf16[8,128,128]{2,1,0:T(8,128)(2,1)S(1)}, bf16[8,128,128]{2,1,0:T(8,128)(2,1)S(1)}, u32[]{:S(2)}, u32[]{:S(2)}) collective-permute-start(bf16[8,128,128]{2,1,0:T(8,128)(2,1)S(1)} %slice.4), channel_id=1, source_target_pairs={{8,0},{9,1},{10,2},{11,3},{12,4},{13,5},{14,6},{15,7},{16,12},{17,... | collective-permute-start | bytes 786440 | tf_op jit(solution)/shard_map/ppermute | solution.py:257
  63.8 31.5 %all-to-all-start.2 = ((bf16[4,512,128]{2,1,0:T(8,128)(2,1)}), bf16[4,512,128]{2,1,0:T(8,128)(2,1)S(1)}, u32[]{:S(2)}, u32[]{:S(2)}) async-start(bf16[4,512,128]{2,1,0:T(8,128)(2,1)} %stack.3), calls=%async_computation.2 | async-start | bytes 1048576 | tf_op jit(solution)/shard_map/all_to_all | solution.py:263
  71.6 11.0 %collective-permute-start.1 = (bf16[512,128]{1,0:T(8,128)(2,1)S(1)}, bf16[512,128]{1,0:T(8,128)(2,1)S(1)}, u32[]{:S(2)}, u32[]{:S(2)}) collective-permute-start(bf16[512,128]{1,0:T(8,128)(2,1)S(1)} %get-tuple-element.13), channel_id=1, source_target_pairs={{0,1},{1,0},{2,3},{3,2},{4,5},{5,4},{6,7},{7,6},{8,9},{9,8},{10,11... | collective-permute-start | bytes 393224 | tf_op jit(solution)/shard_map/ppermute | solution.py:268
  77.6 8.3 %collective-permute-start.2 = (bf16[512,128]{1,0:T(8,128)(2,1)S(1)}, bf16[512,128]{1,0:T(8,128)(2,1)S(1)}, u32[]{:S(2)}, u32[]{:S(2)}) collective-permute-start(bf16[512,128]{1,0:T(8,128)(2,1)S(1)} %get-tuple-element.14), channel_id=1, source_target_pairs={{0,2},{1,3},{2,0},{3,1},{4,6},{5,7},{6,4},{7,5},{8,10},{9,11},{10,... | collective-permute-start | bytes 393224 | tf_op jit(solution)/shard_map/ppermute | solution.py:268
  79.5 15.8 %collective-permute-start.3 = (bf16[512,128]{1,0:T(8,128)(2,1)S(1)}, bf16[512,128]{1,0:T(8,128)(2,1)S(1)}, u32[]{:S(2)}, u32[]{:S(2)}) collective-permute-start(bf16[512,128]{1,0:T(8,128)(2,1)S(1)} %get-tuple-element.15), channel_id=1, source_target_pairs={{0,3},{1,2},{2,1},{3,0},{4,7},{5,6},{6,5},{7,4},{8,11},{9,10},{10,... | collective-permute-start | bytes 393224 | tf_op jit(solution)/shard_map/ppermute | solution.py:268

commit v6 on v5

--- a/solution.py
+++ b/solution.py
@@ -227,7 +227,7 @@
 
 
 def turn_pieces(pieces, sub):
-    steps = 2
+    steps = 4
     return pl.pallas_call(
         turn_kernel,
         out_shape=jax.ShapeDtypeStruct((sub, OFFS, 2 * BINS), BF16),

time: 97.4 us -> 98.1 us (level)
  no operation moved by 1% of the time
where the time goes in v6:
time: 98.1 us; the launch traced here: 97.6 us
  starting transfers between devices  31.8 us (32%)
  waiting for transfers between devices  29.5 us (30%)
  blocking collectives  25 us (25%)
  Pallas kernels  11.2 us (11%)
    all_to_all x1, blocking collectives, shards(): lax.all_to_all(message, ('h', 'q'), 0, 0, tiled=True)  25 us
    all_to_all x1, waiting for transfers between devices, shards(): lax.all_to_all(message, ('h', 'q'), 0, 0, tiled=True)  15.4 us
    ppermute x3, waiting for transfers between devices, shards(): part[slot] = lax.ppermute(stacked[slot], axes, pairs)  12.7 us
    ppermute x3, starting transfers between devices, shards(): part[slot] = lax.ppermute(stacked[slot], axes, pairs)  11 us
    ppermute x2, starting transfers between devices, shards(): halos = [lax.ppermute(own[:, -GROUP * 8:], axes, behind) for own in owns]  8.11 us
    all_to_all x1, starting transfers between devices, shards(): lax.all_to_all(message, ('h', 'q'), 0, 0, tiled=True)  7.94 us
    pallas_call x1, Pallas kernels, spectra(): pl.pallas_call(functools.partial(spectrum_kernel, nsamp), out_shape=[jax....  4.82 us
    all_to_all x1, starting transfers between devices, shards(): pieces.append(lax.all_to_all(stacked[0], 'q', 0, 0, tiled=True))  4.74 us
  transfers between devices with their start and end apart: 7, of which 4 were waited for; matrix products, arithmetic and copies ran while one was open for 0% of the time, Pallas kernels for 4%

profile of v6, /device:TPU:81, one launch (start us, length us, event | category | flops | bytes accessed | tf_op | source)
XLA Modules:
  0.0 97.6 jit_solution(9946569250188067549)
XLA Ops:
  0.0 4.8 %spectra.1 = (bf16[8,144,128]{2,1,0:T(8,128)(2,1)}, bf16[8,128,128]{2,1,0:T(8,128)(2,1)}) custom-call(s32[4]{0:T(128)} %use_ref.1, s32[1,128]{1,0:T(1,128)} %bitcast.1, bf16[128,4,3072]{2,1,0:T(4,128)(2,1)} %raw_ref.1, bf16[3072,256]{1,0:T(8,128)(2,1)} %constant.2.clone.basis_ref), custom_call_target="tpu_custom_call" | custom-call | tf_op jit(solution)/shard_map/spectra/pallas_call | solution.py:188
  4.8 25.0 %all_to_all.15.own_ref = bf16[8,128,128]{2,1,0:T(8,128)(2,1)S(1)} all-to-all(bf16[8,128,128]{2,1,0:T(8,128)(2,1)} %get-tuple-element.16), channel_id=1, replica_groups=mesh['chan'=64,'h'=2,'q'=4] {'h','q'}, dimensions={0} | all-to-all | bytes 524288 | tf_op jit(solution)/shard_map/all_to_all | solution.py:256
  29.8 7.9 %all-to-all-start = ((bf16[8,144,128]{2,1,0:T(8,128)(2,1)}), bf16[8,144,128]{2,1,0:T(8,128)(2,1)S(1)}, u32[]{:S(2)}, u32[]{:S(2)}) async-start(bf16[8,144,128]{2,1,0:T(8,128)(2,1)} %get-tuple-element.11), calls=%async_computation | async-start | bytes 589824 | tf_op jit(solution)/shard_map/all_to_all | solution.py:256
  37.8 3.6 %collective-permute-start.4 = (bf16[8,128,128]{2,1,0:T(8,128)(2,1)S(1)}, bf16[8,128,128]{2,1,0:T(8,128)(2,1)S(1)}, u32[]{:S(2)}, u32[]{:S(2)}) collective-permute-start(bf16[8,128,128]{2,1,0:T(8,128)(2,1)S(1)} %all_to_all.15.own_ref), channel_id=1, source_target_pairs={{8,0},{9,1},{10,2},{11,3},{12,4},{13,5},{14,6},{15,7},{16,12},{17,... | collective-permute-start | bytes 786440 | tf_op jit(solution)/shard_map/ppermute | solution.py:257
  41.3 15.4 %all-to-all-done.own_ref.flag_ref = bf16[8,144,128]{2,1,0:T(8,128)(2,1)S(1)} async-done(((bf16[8,144,128]{2,1,0:T(8,128)(2,1)}), bf16[8,144,128]{2,1,0:T(8,128)(2,1)S(1)}, u32[]{:S(2)}, u32[]{:S(2)}) %all-to-all-start) | async-done | bytes 294944 | tf_op jit(solution)/shard_map/all_to_all | solution.py:256
  56.8 4.6 %collective-permute-start = (bf16[8,128,128]{2,1,0:T(8,128)(2,1)S(1)}, bf16[8,128,128]{2,1,0:T(8,128)(2,1)S(1)}, u32[]{:S(2)}, u32[]{:S(2)}) collective-permute-start(bf16[8,128,128]{2,1,0:T(8,128)(2,1)S(1)} %slice.4), channel_id=1, source_target_pairs={{8,0},{9,1},{10,2},{11,3},{12,4},{13,5},{14,6},{15,7},{16,12},{17,... | collective-permute-start | bytes 786440 | tf_op jit(solution)/shard_map/ppermute | solution.py:257
  61.3 0.0 collective-permute-done.4.halo_ref
  61.4 2.5 %stack.3 = bf16[4,512,128]{2,1,0:T(8,128)(2,1)} custom-call(bf16[8,128,128]{2,1,0:T(8,128)(2,1)S(1)} %all_to_all.15.own_ref, bf16[8,128,128]{2,1,0:T(8,128)(2,1)S(1)} %collective-permute-done.4.halo_ref, bf16[8,144,128]{2,1,0:T(8,128)(2,1)S(1)} %all-to-all-done.own_ref.flag_ref), custom_call_target="tpu_custom_call" | custom-call | flops 26843545600 | bytes 104857600 | tf_op jit(solution)/shard_map/stack/pallas_call | solution.py:217
  63.8 4.7 %all-to-all-start.2 = ((bf16[4,512,128]{2,1,0:T(8,128)(2,1)}), bf16[4,512,128]{2,1,0:T(8,128)(2,1)S(1)}, u32[]{:S(2)}, u32[]{:S(2)}) async-start(bf16[4,512,128]{2,1,0:T(8,128)(2,1)} %stack.3), calls=%async_computation.2 | async-start | bytes 1048576 | tf_op jit(solution)/shard_map/all_to_all | solution.py:263
  68.6 1.3 %collective-permute-done.halo_ref = bf16[8,128,128]{2,1,0:T(8,128)(2,1)S(1)} collective-permute-done((bf16[8,128,128]{2,1,0:T(8,128)(2,1)S(1)}, bf16[8,128,128]{2,1,0:T(8,128)(2,1)S(1)}, u32[]{:S(2)}, u32[]{:S(2)}) %collective-permute-start) | collective-permute-done | bytes 262176 | tf_op jit(solution)/shard_map/ppermute | solution.py:257
  69.9 1.7 %stack.2 = (bf16[512,128]{1,0:T(8,128)(2,1)S(1)}, bf16[512,128]{1,0:T(8,128)(2,1)S(1)}, bf16[512,128]{1,0:T(8,128)(2,1)S(1)}, bf16[512,128]{1,0:T(8,128)(2,1)S(1)}) custom-call(bf16[8,144,128]{2,1,0:T(8,128)(2,1)S(1)} %all-to-all-done.own_ref.flag_ref, bf16[8,128,128]{2,1,0:T(8,128)(2,1)S(1)} %collective-permute-done.halo_ref, ...), custom_call_target="tpu_custom_call" | custom-call | flops 26843545600 | bytes 104857600 | tf_op jit(solution)/shard_map/stack/pallas_call | solution.py:217
  71.6 6.0 %collective-permute-start.1 = (bf16[512,128]{1,0:T(8,128)(2,1)S(1)}, bf16[512,128]{1,0:T(8,128)(2,1)S(1)}, u32[]{:S(2)}, u32[]{:S(2)}) collective-permute-start(bf16[512,128]{1,0:T(8,128)(2,1)S(1)} %get-tuple-element.13), channel_id=1, source_target_pairs={{0,1},{1,0},{2,3},{3,2},{4,5},{5,4},{6,7},{7,6},{8,9},{9,8},{10,11... | collective-permute-start | bytes 393224 | tf_op jit(solution)/shard_map/ppermute | solution.py:268
  77.6 1.9 %collective-permute-start.2 = (bf16[512,128]{1,0:T(8,128)(2,1)S(1)}, bf16[512,128]{1,0:T(8,128)(2,1)S(1)}, u32[]{:S(2)}, u32[]{:S(2)}) collective-permute-start(bf16[512,128]{1,0:T(8,128)(2,1)S(1)} %get-tuple-element.14), channel_id=1, source_target_pairs={{0,2},{1,3},{2,0},{3,1},{4,6},{5,7},{6,4},{7,5},{8,10},{9,11},{10,... | collective-permute-start | bytes 393224 | tf_op jit(solution)/shard_map/ppermute | solution.py:268
  79.5 3.1 %collective-permute-start.3 = (bf16[512,128]{1,0:T(8,128)(2,1)S(1)}, bf16[512,128]{1,0:T(8,128)(2,1)S(1)}, u32[]{:S(2)}, u32[]{:S(2)}) collective-permute-start(bf16[512,128]{1,0:T(8,128)(2,1)S(1)} %get-tuple-element.15), channel_id=1, source_target_pairs={{0,3},{1,2},{2,1},{3,0},{4,7},{5,6},{6,5},{7,4},{8,11},{9,10},{10,... | collective-permute-start | bytes 393224 | tf_op jit(solution)/shard_map/ppermute | solution.py:268
  82.6 0.0 collective-permute-done.1.refs_1_
  82.6 3.3 %collective-permute-done.2.refs_2_ = bf16[512,128]{1,0:T(8,128)(2,1)S(1)} collective-permute-done((bf16[512,128]{1,0:T(8,128)(2,1)S(1)}, bf16[512,128]{1,0:T(8,128)(2,1)S(1)}, u32[]{:S(2)}, u32[]{:S(2)}) %collective-permute-start.2) | collective-permute-done | bytes 131104 | tf_op jit(solution)/shard_map/ppermute | solution.py:268
  85.9 9.4 %collective-permute-done.3.refs_3_ = bf16[512,128]{1,0:T(8,128)(2,1)S(1)} collective-permute-done((bf16[512,128]{1,0:T(8,128)(2,1)S(1)}, bf16[512,128]{1,0:T(8,128)(2,1)S(1)}, u32[]{:S(2)}, u32[]{:S(2)}) %collective-permute-start.3) | collective-permute-done | bytes 131104 | tf_op jit(solution)/shard_map/ppermute | solution.py:268
  95.3 0.0 all-to-all-done.2.refs_4_
  95.3 2.3 %turn.1 = bf16[16,128,256]{2,1,0:T(8,128)(2,1)} custom-call(bf16[512,128]{1,0:T(8,128)(2,1)S(1)} %get-tuple-element.12.refs_0_, bf16[512,128]{1,0:T(8,128)(2,1)S(1)} %collective-permute-done.1.refs_1_, bf16[512,128]{1,0:T(8,128)(2,1)S(1)} %collective-permute-done.2.refs_2_, bf16[512,128]{1,0:T(8,128)(2,1)S(1)} %collective-permute-done.3.refs_3_, ...), custom_call_target="tpu_custom_call" | custom-call | tf_op jit(solution)/shard_map/turn/pallas_call | solution.py:231
  (1 shorter events, 0.0 us)
Async XLA Ops:
  29.8 26.9 %all-to-all-start = ((bf16[8,144,128]{2,1,0:T(8,128)(2,1)}), bf16[8,144,128]{2,1,0:T(8,128)(2,1)S(1)}, u32[]{:S(2)}, u32[]{:S(2)}) async-start(bf16[8,144,128]{2,1,0:T(8,128)(2,1)} %get-tuple-element.11), calls=%async_computation | async-start | bytes 589824 | tf_op jit(solution)/shard_map/all_to_all | solution.py:256
  37.8 23.6 %collective-permute-start.4 = (bf16[8,128,128]{2,1,0:T(8,128)(2,1)S(1)}, bf16[8,128,128]{2,1,0:T(8,128)(2,1)S(1)}, u32[]{:S(2)}, u32[]{:S(2)}) collective-permute-start(bf16[8,128,128]{2,1,0:T(8,128)(2,1)S(1)} %all_to_all.15.own_ref), channel_id=1, source_target_pairs={{8,0},{9,1},{10,2},{11,3},{12,4},{13,5},{14,6},{15,7},{16,12},{17,... | collective-permute-start | bytes 786440 | tf_op jit(solution)/shard_map/ppermute | solution.py:257
  56.8 13.1 %collective-permute-start = (bf16[8,128,128]{2,1,0:T(8,128)(2,1)S(1)}, bf16[8,128,128]{2,1,0:T(8,128)(2,1)S(1)}, u32[]{:S(2)}, u32[]{:S(2)}) collective-permute-start(bf16[8,128,128]{2,1,0:T(8,128)(2,1)S(1)} %slice.4), channel_id=1, source_target_pairs={{8,0},{9,1},{10,2},{11,3},{12,4},{13,5},{14,6},{15,7},{16,12},{17,... | collective-permute-start | bytes 786440 | tf_op jit(solution)/shard_map/ppermute | solution.py:257
  63.8 31.5 %all-to-all-start.2 = ((bf16[4,512,128]{2,1,0:T(8,128)(2,1)}), bf16[4,512,128]{2,1,0:T(8,128)(2,1)S(1)}, u32[]{:S(2)}, u32[]{:S(2)}) async-start(bf16[4,512,128]{2,1,0:T(8,128)(2,1)} %stack.3), calls=%async_computation.2 | async-start | bytes 1048576 | tf_op jit(solution)/shard_map/all_to_all | solution.py:263
  71.6 11.0 %collective-permute-start.1 = (bf16[512,128]{1,0:T(8,128)(2,1)S(1)}, bf16[512,128]{1,0:T(8,128)(2,1)S(1)}, u32[]{:S(2)}, u32[]{:S(2)}) collective-permute-start(bf16[512,128]{1,0:T(8,128)(2,1)S(1)} %get-tuple-element.13), channel_id=1, source_target_pairs={{0,1},{1,0},{2,3},{3,2},{4,5},{5,4},{6,7},{7,6},{8,9},{9,8},{10,11... | collective-permute-start | bytes 393224 | tf_op jit(solution)/shard_map/ppermute | solution.py:268
  77.6 8.3 %collective-permute-start.2 = (bf16[512,128]{1,0:T(8,128)(2,1)S(1)}, bf16[512,128]{1,0:T(8,128)(2,1)S(1)}, u32[]{:S(2)}, u32[]{:S(2)}) collective-permute-start(bf16[512,128]{1,0:T(8,128)(2,1)S(1)} %get-tuple-element.14), channel_id=1, source_target_pairs={{0,2},{1,3},{2,0},{3,1},{4,6},{5,7},{6,4},{7,5},{8,10},{9,11},{10,... | collective-permute-start | bytes 393224 | tf_op jit(solution)/shard_map/ppermute | solution.py:268
  79.5 15.8 %collective-permute-start.3 = (bf16[512,128]{1,0:T(8,128)(2,1)S(1)}, bf16[512,128]{1,0:T(8,128)(2,1)S(1)}, u32[]{:S(2)}, u32[]{:S(2)}) collective-permute-start(bf16[512,128]{1,0:T(8,128)(2,1)S(1)} %get-tuple-element.15), channel_id=1, source_target_pairs={{0,3},{1,2},{2,1},{3,0},{4,7},{5,6},{6,5},{7,4},{8,11},{9,10},{10,... | collective-permute-start | bytes 393224 | tf_op jit(solution)/shard_map/ppermute | solution.py:268
